TPU v7x, 128 devices: a whole 4x4x4 slice. The times are simulated.
128 devices in a mesh: row: 16 (over y, z), col: 8 (over x, core).
Axes of the slice: x: 4, y: 4, z: 4, core: 2. Of those that a mesh axis runs over, the one named last changes fastest.
Arguments:
- trailing_block: float32 [2, 16, 512, 4, 8, 512], P(None, 'row', None, None, 'col'), may hold values from -6 to 6
- panel_block: float32 [2, 16, 512, 1024], P(None, 'row', None, 'col'), may hold values from -0.9 to 0.9
- inv_factor: float32 [1024, 1024], replicated, as said below
Outputs:
- updated: float32 [2, 16, 512, 4, 8, 512], P(None, 'row', None, None, 'col')
- factor_panel: float32 [2, 16, 512, 1024], P(None, 'row', None, 'col')
Inputs may be any that keep to these rules, and one draw needn't show every extreme that they name: `inv_factor`: lower triangular; diagonal entries lie between 1 and 2.
All inputs are finite; a program needn't handle non-finite values.
Results may differ from a plain program's by a relative error of at most 0.00007.
Values sent between devices are 32-bit elements; how exact they have to be, the bound alone decides.
No kernel may reach another device: no remote copies, remote signals or barrier semaphores. Data moves between devices by JAX's collectives and lax.ppermute only.
A program may use at most 128 MiB of HBM per device.

v0:
```python
import jax
import jax.numpy as jnp
from jax import lax
from jax.sharding import PartitionSpec as P


def broadcast(block, axis, source):
    block = jnp.where(lax.axis_index(axis) == source, block, jnp.zeros_like(block))
    return lax.psum(block, axis)


def contract_last(left, right):
    return lax.dot_general(
        left,
        right,
        (((1,), (1,)), ((), ())),
        precision=lax.Precision.HIGHEST,
        preferred_element_type=jnp.float32,
    )


def per_device(trailing_block, panel_block, inv_factor):
    rt_count, _, tile_size, cols_dev = panel_block.shape
    ct_count = trailing_block.shape[3]
    full_cols = inv_factor.shape[0]
    share_count = lax.axis_size("row") // lax.axis_size("col")
    local_rows = rt_count * tile_size
    col_index = lax.axis_index("col")
    shard_part = lax.all_gather(panel_block, "col", axis=3, tiled=True)
    shard_cols = shard_part.shape[3]
    factor_rows = contract_last(shard_part.reshape(local_rows, shard_cols), inv_factor)
    received = []
    for offset in range(share_count):
        source_row = offset * lax.axis_size("col") + col_index
        received.append(broadcast(factor_rows, "row", source_row))
    stacked = jnp.stack(
        [message.reshape(rt_count, tile_size, full_cols) for message in received], axis=1
    )
    column_rows = stacked.reshape(ct_count * tile_size, full_cols)
    product = contract_last(factor_rows, column_rows)
    own_columns = lax.dynamic_slice_in_dim(factor_rows, col_index * cols_dev, cols_dev, 1)
    updated = trailing_block.reshape(local_rows, ct_count * tile_size) - product
    return (updated.reshape(trailing_block.shape), own_columns.reshape(panel_block.shape))


def solution(mesh):
    return jax.shard_map(
        per_device,
        mesh=mesh,
        in_specs=(P(None, "row", None, None, "col", None), P(None, "row", None, "col"), P()),
        out_specs=(P(None, "row", None, None, "col", None), P(None, "row", None, "col")),
        check_vma=False,
    )
```

profile of v0, /device:TPU:6, one launch (start us, length us, event | category | flops | bytes accessed | tf_op | source)
XLA Modules:
  0.0 267.5 jit_solution(16521010896470110737)
XLA Ops:
  7.2 0.0 all-gather.2.cloned.1.call-start
  7.2 0.7 all-gather.2.cloned.1.call-update
  7.9 0.0 all-reduce.3.cloned.1.call-start
  8.0 39.5 %all-gather.2.cloned.1.call-done = f32[2,1,512,1024]{3,2,1,0:T(8,128)} async-done(((f32[2,1,512,128]{3,2,1,0:T(8,128)}), f32[2,1,512,1024]{3,2,1,0:T(8,128)}) %all-gather.2.cloned.1.call-update) | async-done | bytes 4194320 | tf_op jit(solution)/shard_map/all_gather | solution.py:29
  47.4 19.3 %broadcast_select_fusion.1 = (f32[1024,1024]{1,0:T(8,128)}, f32[1024,1024]{1,0:T(8,128)}, f32[1024,1024]{1,0:T(8,128)}) fusion(pred[]{:T(512)S(6)} %eq.6, pred[]{:T(512)S(6)} %eq.7, f32[1024,1024]{1,0:T(8,128)} %bitcast.21, f32[1024,1024]{1,0:T(8,128)} %param.5), kind=kOutput, calls=%fused_computation.3 | convolution fusion | flops 12886999040 | bytes 20971522 | tf_op jit(solution)/shard_map/dot_general | solution.py:13
  66.7 0.0 all-reduce.3.cloned.1.call-update
  66.7 26.9 %reduce = f32[2,512,4,512]{3,2,1,0:T(4,128)} reduce(f32[2,1,512,4,1,512]{5,4,3,2,1,0:T(1,128)} %param.3, f32[]{:T(128)} %constant.21), dimensions={1,4}, to_apply=%param.3.reduce_sub_computation | reduce | bytes 16777220 | tf_op args[0]
  93.6 11.3 %copy.9 = f32[128,8,4,512]{3,1,2,0:T(8,128)} copy(f32[128,8,4,512]{3,2,1,0:T(4,128)} %bitcast.16) | data formatting | bytes 16777216
  104.9 1.9 constant_dynamic-slice_fusion
  106.7 103.9 %all-reduce.3.cloned.1.call-done = (f32[2,1,512,1024]{3,2,1,0:T(8,128)}, f32[2,1,512,1024]{3,2,1,0:T(8,128)}) async-done(((f32[2,1,512,1024]{3,2,1,0:T(8,128)}, f32[2,1,512,1024]{3,2,1,0:T(8,128)}), (f32[2,1,512,1024]{3,2,1,0:T(8,128)}, f32[2,1,512,1024]{3,2,1,0:T(8,128)})) %all-reduce.3.cloned.1.call-update) | async-done | bytes 8388624 | tf_op jit(solution)/shard_map/psum | solution.py:9
  210.7 0.0 copy-start
  210.7 0.0 copy-start.1
  210.7 4.5 %pad_maximum_fusion = f32[2,2,512,1024]{3,2,1,0:T(8,128)S(1)} fusion(f32[2,1,512,1024]{3,2,1,0:T(8,128)} %get-tuple-element.6, f32[2,1,512,1024]{3,2,1,0:T(8,128)} %get-tuple-element.7), kind=kLoop, calls=%fused_computation | loop fusion | flops 2097152 | bytes 16777216 | tf_op jit(solution)/shard_map/stack | solution.py:36
  215.2 1.3 copy-done
  216.5 1.2 copy-done.1
  217.7 29.4 %convolution_subtract_fusion = f32[1024,2048]{1,0:T(8,128)} fusion(f32[1024,2048]{1,0:T(8,128)S(1)} %bitcast.19, f32[1024,1024]{1,0:T(8,128)S(1)} %copy-done.1, f32[2048,1024]{1,0:T(8,128)S(1)} %bitcast.20), kind=kOutput, calls=%fused_computation.1 | convolution fusion | flops 25771900928 | bytes 29360128 | tf_op jit(solution)/shard_map/dot_general | solution.py:13
  247.1 13.5 %reshape.24 = f32[2,1,512,4,1,512]{5,4,3,2,1,0:T(1,128)} reshape(f32[1024,2048]{1,0:T(8,128)} %convolution_subtract_fusion) | data formatting | bytes 16777216 | tf_op jit(solution)/shard_map/reshape | solution.py:43
Async XLA Ops:
  7.2 40.3 %all-gather.2.cloned.1.call-start = ((), (), s32[]{:S(2)}) async-start(), calls=%async_computation | async-start | bytes 4718592 | tf_op jit(solution)/shard_map/all_gather | solution.py:29
  7.9 202.8 %all-reduce.3.cloned.1.call-start = ((), (), s32[]{:S(2)}) async-start(), calls=%async_computation.1 | async-start | bytes 16777216 | tf_op jit(solution)/shard_map/psum | solution.py:9
  210.7 5.8 %copy-start = (f32[128,8,4,512]{3,1,2,0:T(8,128)S(1)}, f32[128,8,4,512]{3,1,2,0:T(8,128)}, u32[]{:S(2)}) copy-start(f32[128,8,4,512]{3,1,2,0:T(8,128)} %copy.9) | copy-start | bytes 25165828
  210.7 7.0 %copy-start.1 = (f32[1024,1024]{1,0:T(8,128)S(1)}, f32[1024,1024]{1,0:T(8,128)}, u32[]{:S(2)}) copy-start(f32[1024,1024]{1,0:T(8,128)} %get-tuple-element.10) | copy-start | bytes 12582916
Sparse Core Ops, SparseCore 0:
  9.7 37.6 all-gather.1
  66.8 143.8 all-reduce.2
where the time goes:
time: 268 us; the launch traced here: 267 us
  waiting for transfers between devices  144 us (54%)
  matrix products  48.7 us (18%)
  other arithmetic  31.4 us (12%)
  local copies, waits for them, and re-layouts  29.1 us (11%)
  between operations  14.1 us (5%)
    psum x1, waiting for transfers between devices, broadcast(): return lax.psum(block, axis)  104 us
    dot_general x2, matrix products, contract_last(): lax.dot_general(left, right, (((1,), (1,)), ((), ())), precision=lax.Prec...  48.7 us
    all_gather x1, waiting for transfers between devices, per_device(): shard_part = lax.all_gather(panel_block, 'col', axis=3, tiled=True)  39.5 us
    unnamed x1, other arithmetic  26.9 us
    unnamed x5, local copies, waits for them, and re-layouts  13.8 us
    reshape x1, local copies, waits for them, and re-layouts, per_device(): updated.reshape(trailing_block.shape)  13.5 us
  transfers between devices with their start and end apart: 2, of which 2 were waited for; matrix products, arithmetic and copies ran while one was open for 15% of the time, Pallas kernels for 0%

commit v1 on v0

v1 whole, which is shorter than its diff:
```python
import functools

import jax
import jax.numpy as jnp
from jax import lax
from jax.experimental import pallas as pl
from jax.experimental.pallas import tpu as pltpu
from jax.sharding import PartitionSpec as P

BOTH = ("row", "col")
F32, BF16 = jnp.float32, jnp.bfloat16
LAST = (((1,), (1,)), ((), ()))
PLAIN = (((1,), (0,)), ((), ()))
VMEM_LIMIT = 56 * 1024 * 1024


def device_index(x, y, z, core):
    return (y * 4 + z) * 8 + x * 2 + core


def permutation(move):
    pairs = []
    for x in range(4):
        for y in range(4):
            for z in range(4):
                for core in range(2):
                    to_y, to_z = move(y, z, core)
                    pairs.append(
                        (device_index(x, y, z, core), device_index(x, to_y % 4, to_z % 4, core))
                    )
    return pairs


def first_axis(step):
    return permutation(lambda y, z, core: (y, z + step) if core == 0 else (y + step, z))


def second_axis(step):
    return permutation(lambda y, z, core: (y + step, z) if core == 0 else (y, z + step))


def spread():
    pairs = []
    for half in range(2):
        for k in range(8):
            for c in range(8):
                pairs.append(((8 * half + c) * 8 + k, (8 * half + k) * 8 + c))
    return pairs


def ring(block, axis):
    rows = block.shape[0] // 2
    ahead = lax.ppermute(block, BOTH, axis(-1))
    behind = lax.ppermute(block, BOTH, axis(1))
    far_top = lax.ppermute(ahead[:rows], BOTH, axis(-1))
    far_bottom = lax.ppermute(behind[rows:], BOTH, axis(1))
    return ahead, behind, far_top, far_bottom


def split(value):
    high = value.astype(BF16)
    return high, (value - high.astype(F32)).astype(BF16)


def dot3(left, right, dims):
    dot = functools.partial(lax.dot_general, dimension_numbers=dims, preferred_element_type=F32)
    return dot(left[0], right[0]) + (dot(left[0], right[1]) + dot(left[1], right[0]))


def factor_kernel(col_ref, rows_ref, inv_ref, own_ref, ghi_ref, glo_ref, f_ref, bhi, blo, lhi, llo):
    wide = 256
    count = inv_ref.shape[0] // wide
    for k in range(2 * count):
        high, low = split(rows_ref[k])
        bhi[:, k * 128 : (k + 1) * 128] = high
        blo[:, k * 128 : (k + 1) * 128] = low
    high, low = split(inv_ref[...])
    lhi[...] = high
    llo[...] = low

    def cut(at):
        return slice(at * wide, (at + 1) * wide)

    for j in range(count):
        upto = slice(0, (j + 1) * wide)
        f_ref[:, cut(j)] = dot3(
            (bhi[:, upto], blo[:, upto]), (lhi[cut(j), upto], llo[cut(j), upto]), LAST
        )
    start = pl.multiple_of(col_ref[0] * 128, 128)
    own_ref[...] = f_ref[:, pl.ds(start, 128)]
    high, low = split(f_ref[...])
    bhi[...] = high
    blo[...] = low
    for k in range(count):
        onward = slice(k * wide, count * wide)
        total = dot3(
            (bhi[:, onward], blo[:, onward]), (lhi[onward, cut(k)], llo[onward, cut(k)]), PLAIN
        )
        high, low = split(total)
        ghi_ref[:, cut(k)] = high
        glo_ref[:, cut(k)] = low


def factor(col_index, rows, inv_factor):
    count, local, _ = rows.shape
    order = inv_factor.shape[0]
    vmem = pl.BlockSpec(memory_space=pltpu.VMEM)
    return pl.pallas_call(
        factor_kernel,
        out_shape=(
            jax.ShapeDtypeStruct((local, 128), F32),
            jax.ShapeDtypeStruct((local, order), BF16),
            jax.ShapeDtypeStruct((local, order), BF16),
        ),
        in_specs=[pl.BlockSpec(memory_space=pltpu.SMEM), vmem, vmem],
        out_specs=(vmem, vmem, vmem),
        scratch_shapes=[
            pltpu.VMEM((local, order), F32),
            pltpu.VMEM((local, order), BF16),
            pltpu.VMEM((local, order), BF16),
            pltpu.VMEM((order, order), BF16),
            pltpu.VMEM((order, order), BF16),
        ],
        compiler_params=pltpu.CompilerParams(vmem_limit_bytes=VMEM_LIMIT),
        cost_estimate=pl.CostEstimate(
            flops=2 * 3 * local * order * order, bytes_accessed=13 * 2**20, transcendentals=0
        ),
    )(col_index, rows, inv_factor)


def update_kernel(place_ref, ghi, glo, held, ahead, behind, top, bottom, a_ref, *rest):
    out_ref, b_ref, bhi, blo, sems = rest[-5:]
    block_rows = a_ref.shape[0]
    tile = 512

    @pl.when(pl.program_id(0) == 0)
    def _():
        copies = []
        for ref in (held, ahead, behind, top, bottom):
            for part in range(ref.shape[0] // tile):
                at = len(copies)
                place = place_ref[at]
                row = pl.multiple_of((place // 8) * tile, tile)
                lane = pl.multiple_of((place % 8) * 128, 128)
                copy = pltpu.make_async_copy(
                    ref.at[pl.ds(part * tile, tile), :],
                    b_ref.at[pl.ds(row, tile), pl.ds(lane, 128)],
                    sems.at[at],
                )
                copy.start()
                copies.append(copy)
        for copy in copies:
            copy.wait()
        high, low = split(b_ref[...])
        bhi[...] = high
        blo[...] = low

    a_rows = a_ref.reshape(block_rows * 8, 128)
    out_rows = out_ref.reshape(block_rows * 8, 128)
    for n in range(4):
        cols = slice(n * 256, (n + 1) * 256)
        product = dot3((ghi[...], glo[...]), (bhi[cols, :], blo[cols, :]), LAST)
        for j in range(2):
            lines = pl.ds(2 * n + j, block_rows, 8)
            out_rows[lines, :] = a_rows[lines, :] - product[:, j * 128 : (j + 1) * 128]


def update(part, place, g, received, trailing, so_far):
    local, order = g[0].shape
    block_rows = 256
    g_spec = pl.BlockSpec((block_rows, order), lambda i, place: (i, 0))
    a_spec = pl.BlockSpec((block_rows, 8, 128), lambda i, place: (i, part, 0))
    hbm = pl.BlockSpec(memory_space=pl.ANY)
    operands = [place, *g, *received, trailing]
    in_specs = [g_spec, g_spec, *[hbm] * len(received), a_spec]
    aliases = {}
    if so_far is not None:
        aliases = {len(operands): 0}
        operands.append(so_far)
        in_specs.append(hbm)
    return pl.pallas_call(
        update_kernel,
        out_shape=jax.ShapeDtypeStruct(trailing.shape, F32),
        grid_spec=pltpu.PrefetchScalarGridSpec(
            num_scalar_prefetch=1,
            grid=(local // block_rows,),
            in_specs=in_specs,
            out_specs=a_spec,
            scratch_shapes=[
                pltpu.VMEM((1024, order), F32),
                pltpu.VMEM((1024, order), BF16),
                pltpu.VMEM((1024, order), BF16),
                pltpu.SemaphoreType.DMA((16,)),
            ],
        ),
        input_output_aliases=aliases,
        compiler_params=pltpu.CompilerParams(vmem_limit_bytes=VMEM_LIMIT),
        cost_estimate=pl.CostEstimate(
            flops=2 * 3 * local * 1024 * order, bytes_accessed=16 * 2**20, transcendentals=0
        ),
    )(*operands)


def places():
    row, core = lax.axis_index("row"), lax.axis_index("col") % 2
    y, z = row // 4, row % 4
    order = [(0, s) for s in range(4)] + [(1, s) for s in range(4)]
    order += [(3, s) for s in range(4)] + [(2, s) for s in range(4)]
    steps = (0, 1, 3, 2)
    second = jnp.array([d for d, _ in order], jnp.int32)
    first = jnp.array([steps[s] for _, s in order], jnp.int32)
    at_y = (y + jnp.where(core == 0, second, first)) % 4
    at_z = (z + jnp.where(core == 0, first, second)) % 4
    return at_y * 4 + at_z


def per_device(trailing_block, panel_block, inv_factor):
    tiles, _, tile, cols_dev = panel_block.shape
    local = tiles * tile
    panel = panel_block.reshape(tiles, tile, cols_dev)
    trailing = trailing_block.reshape(local, 16, 128)
    col_index = lax.axis_index("col").astype(jnp.int32).reshape(1)
    rows = lax.all_gather(panel.reshape(local, cols_dev), "col", axis=0)
    place = places()
    received = []
    for part in range(tiles):
        own = lax.ppermute(panel[part], BOTH, spread())
        held = jnp.concatenate([own, *ring(own, first_axis)], axis=0)
        received.append((held, *ring(held, second_axis)))
    own_columns, *g = factor(col_index, rows, inv_factor)
    updated = None
    for part in range(tiles):
        updated = update(part, place, g, received[part], trailing, updated)
    return updated.reshape(trailing_block.shape), own_columns.reshape(panel_block.shape)


def solution(mesh):
    return jax.shard_map(
        per_device,
        mesh=mesh,
        in_specs=(P(None, "row", None, None, "col", None), P(None, "row", None, "col"), P()),
        out_specs=(P(None, "row", None, None, "col", None), P(None, "row", None, "col")),
        check_vma=False,
    )
```

time: 268 us -> 151 us (0.56)
  waiting for transfers between devices: 144 us -> 43.4 us
  matrix products: 48.7 us -> 0 us
  Pallas kernels: 0 us -> 44 us
  starting transfers between devices: 0.08 us -> 36.5 us
  other arithmetic: 31.4 us -> 0.49 us
  local copies, waits for them, and re-layouts: 29.1 us -> 12.7 us
    psum x1 -> x0, waiting for transfers between devices: 104 us -> none  [broadcast(): return lax.psum(block, axis)]
    dot_general x2 -> x0, matrix products: 48.7 us -> none  [contract_last(): lax.dot_general(left, right, (((1,), (1,)), ((), ())), precision=lax.Prec...]
    pallas_call x0 -> x3, Pallas kernels: none -> 44 us  [the longest x2 29.1 us: update(): pl.pallas_call(update_kernel, out_shape=jax.ShapeDtypeStruct(trailing.sha...]
    ppermute x0 -> x18, waiting for transfers between devices: none -> 42.7 us  [the longest x2 28.5 us: per_device(): own = lax.ppermute(panel[part], BOTH, spread())]
    all_gather x1, waiting for transfers between devices: 39.5 us -> 0.01 us  [per_device(): rows = lax.all_gather(panel.reshape(local, cols_dev), 'col', axis=0)]
    ppermute x0 -> x18, starting transfers between devices: none -> 36.5 us  [the longest x4 13 us: ring(): far_top = lax.ppermute(ahead[:rows], BOTH, axis(-1))]
    unnamed x1 -> x0, other arithmetic: 26.9 us -> none
    reshape x1 -> x0, local copies, waits for them, and re-layouts: 13.5 us -> none  [per_device(): updated.reshape(trailing_block.shape)]
  transfers between devices with their start and end apart: 2 -> 19, of which waited for: 2 -> 4; matrix products, arithmetic and copies ran while one was open for 15% -> 9% of each run, Pallas kernels for 0% -> 20%
where the time goes in v1:
time: 151 us
  Pallas kernels  44 us (29%)
  waiting for transfers between devices  43.4 us (29%)
  starting transfers between devices  36.5 us (24%)
  between operations  14.2 us (9%)
  local copies, waits for them, and re-layouts  12.7 us (8%)
    pallas_call x2, Pallas kernels, update(): pl.pallas_call(update_kernel, out_shape=jax.ShapeDtypeStruct(trailing.sha...  29.1 us
    ppermute x2, waiting for transfers between devices, per_device(): own = lax.ppermute(panel[part], BOTH, spread())  28.5 us
    pallas_call x1, Pallas kernels, factor(): pl.pallas_call(factor_kernel, out_shape=(jax.ShapeDtypeStruct((local, 128...  14.9 us
    ppermute x4, waiting for transfers between devices, ring(): behind = lax.ppermute(block, BOTH, axis(1))  14.1 us
    ppermute x4, starting transfers between devices, ring(): far_top = lax.ppermute(ahead[:rows], BOTH, axis(-1))  13 us
    ppermute x4, starting transfers between devices, ring(): ahead = lax.ppermute(block, BOTH, axis(-1))  12.9 us
    ppermute x2, starting transfers between devices, per_device(): own = lax.ppermute(panel[part], BOTH, spread())  10.4 us
    unnamed x18, local copies, waits for them, and re-layouts  5.69 us
  transfers between devices with their start and end apart: 19, of which 4 were waited for; matrix products, arithmetic and copies ran while one was open for 9% of the time, Pallas kernels for 20%

profile of v1, /device:TPU:6, one launch (start us, length us, event | category | flops | bytes accessed | tf_op | source)
XLA Modules:
  0.0 151.2 jit_solution(10163852686191482260)
XLA Ops:
  7.2 0.0 copy-start.3
  7.2 0.0 copy-start.4
  7.2 0.0 all-gather.2.cloned.1.call-start
  7.2 0.7 all-gather.2.cloned.1.call-update
  7.9 1.1 slice_bitcast_fusion
  9.0 6.7 %collective-permute-start.9 = (f32[512,128]{1,0:T(8,128)S(1)}, f32[512,128]{1,0:T(8,128)S(1)}, u32[]{:S(2)}, u32[]{:S(2)}) collective-permute-start(f32[512,128]{1,0:T(8,128)S(1)} %get-tuple-element.12), channel_id=1, source_target_pairs={{0,0},{8,1},{16,2},{24,3},{32,4},{40,5},{48,6},{56,7},{1,8},{9,9},... | collective-permute-start | bytes 786440 | tf_op jit(solution)/shard_map/ppermute | solution.py:227
  15.7 3.6 %collective-permute-start = (f32[512,128]{1,0:T(8,128)S(1)}, f32[512,128]{1,0:T(8,128)S(1)}, u32[]{:S(2)}, u32[]{:S(2)}) collective-permute-start(f32[512,128]{1,0:T(8,128)S(1)} %get-tuple-element.13), channel_id=1, source_target_pairs={{0,0},{8,1},{16,2},{24,3},{32,4},{40,5},{48,6},{56,7},{1,8},{9,9},... | collective-permute-start | bytes 786440 | tf_op jit(solution)/shard_map/ppermute | solution.py:227
  19.4 20.6 %collective-permute-done.9 = f32[512,128]{1,0:T(8,128)S(1)} collective-permute-done((f32[512,128]{1,0:T(8,128)S(1)}, f32[512,128]{1,0:T(8,128)S(1)}, u32[]{:S(2)}, u32[]{:S(2)}) %collective-permute-start.9) | collective-permute-done | bytes 262176 | tf_op jit(solution)/shard_map/ppermute | solution.py:227
  40.0 0.0 collective-permute-start.11
  40.0 3.2 %collective-permute-start.10 = (f32[512,128]{1,0:T(8,128)S(1)}, f32[512,128]{1,0:T(8,128)S(1)}, u32[]{:S(2)}, u32[]{:S(2)}) collective-permute-start(f32[512,128]{1,0:T(8,128)S(1)} %collective-permute-done.9), channel_id=1, source_target_pairs={{0,24},{1,97},{8,0},{9,105},{16,8},{17,113},{24,16},{25,121},{32,5... | collective-permute-start | bytes 786440 | tf_op jit(solution)/shard_map/ppermute | solution.py:53
  43.2 7.9 %collective-permute-done = f32[512,128]{1,0:T(8,128)S(1)} collective-permute-done((f32[512,128]{1,0:T(8,128)S(1)}, f32[512,128]{1,0:T(8,128)S(1)}, u32[]{:S(2)}, u32[]{:S(2)}) %collective-permute-start) | collective-permute-done | bytes 262176 | tf_op jit(solution)/shard_map/ppermute | solution.py:227
  51.1 0.0 collective-permute-start.2
  51.1 3.2 %collective-permute-start.1 = (f32[512,128]{1,0:T(8,128)S(1)}, f32[512,128]{1,0:T(8,128)S(1)}, u32[]{:S(2)}, u32[]{:S(2)}) collective-permute-start(f32[512,128]{1,0:T(8,128)S(1)} %collective-permute-done), channel_id=1, source_target_pairs={{0,24},{1,97},{8,0},{9,105},{16,8},{17,113},{24,16},{25,121},{32,5... | collective-permute-start | bytes 786440 | tf_op jit(solution)/shard_map/ppermute | solution.py:53
  54.3 0.7 constant_dynamic-update-slice_fusion.4
  55.1 0.7 constant_dynamic-update-slice_fusion.9
  55.8 0.0 collective-permute-done.11
  55.8 0.1 collective-permute-start.13
  55.9 0.0 collective-permute-done.10
  55.9 3.3 %collective-permute-start.12 = (f32[256,128]{1,0:T(8,128)S(1)}, f32[256,128]{1,0:T(8,128)S(1)}, u32[]{:S(2)}, u32[]{:S(2)}) collective-permute-start(f32[256,128]{1,0:T(8,128)S(1)} %slice.46), channel_id=1, source_target_pairs={{0,24},{1,97},{8,0},{9,105},{16,8},{17,113},{24,16},{25,121},{32,5... | collective-permute-start | bytes 393224 | tf_op jit(solution)/shard_map/ppermute | solution.py:55
  59.2 0.1 collective-permute-start.4
  59.4 3.3 %collective-permute-start.3 = (f32[256,128]{1,0:T(8,128)S(1)}, f32[256,128]{1,0:T(8,128)S(1)}, u32[]{:S(2)}, u32[]{:S(2)}) collective-permute-start(f32[256,128]{1,0:T(8,128)S(1)} %slice.42), channel_id=1, source_target_pairs={{0,24},{1,97},{8,0},{9,105},{16,8},{17,113},{24,16},{25,121},{32,5... | collective-permute-start | bytes 393224 | tf_op jit(solution)/shard_map/ppermute | solution.py:55
  62.6 0.7 constant_dynamic-update-slice_fusion.3
  63.3 0.7 constant_dynamic-update-slice_fusion.2
  64.1 0.7 constant_dynamic-update-slice_fusion.8
  64.8 0.7 constant_dynamic-update-slice_fusion.7
  65.5 0.7 constant_dynamic-update-slice_fusion.6
  66.2 0.0 collective-permute-done.13
  66.2 0.6 constant_dynamic-update-slice_fusion.5.held
  66.8 0.0 collective-permute-start.15
  66.8 3.2 %collective-permute-start.14 = (f32[2048,128]{1,0:T(8,128)}, f32[2048,128]{1,0:T(8,128)S(1)}, u32[]{:S(2)}, u32[]{:S(2)}) collective-permute-start(f32[2048,128]{1,0:T(8,128)} %constant_dynamic-update-slice_fusion.5.held), channel_id=1, source_target_pairs={{0,96},{1,25},{8,104},{9,1},{16,112},{17,9},{24,120},{25,17},{32,0... | collective-permute-start | bytes 3145736 | tf_op jit(solution)/shard_map/ppermute | solution.py:53
  70.1 0.7 constant_dynamic-update-slice_fusion.1
  70.7 0.0 collective-permute-done.4
  70.7 0.7 constant_dynamic-update-slice_fusion.held
  71.4 3.2 %collective-permute-start.5 = (f32[2048,128]{1,0:T(8,128)}, f32[2048,128]{1,0:T(8,128)}, u32[]{:S(2)}, u32[]{:S(2)}) collective-permute-start(f32[2048,128]{1,0:T(8,128)} %constant_dynamic-update-slice_fusion.held), channel_id=1, source_target_pairs={{0,96},{1,25},{8,104},{9,1},{16,112},{17,9},{24,120},{25,17},{32,0... | collective-permute-start | bytes 3145736 | tf_op jit(solution)/shard_map/ppermute | solution.py:53
  74.6 0.5 fusion.place_ref
  75.1 7.9 %collective-permute-done.15.behind = f32[2048,128]{1,0:T(8,128)S(1)} collective-permute-done((f32[2048,128]{1,0:T(8,128)}, f32[2048,128]{1,0:T(8,128)S(1)}, u32[]{:S(2)}, u32[]{:S(2)}) %collective-permute-start.15) | collective-permute-done | bytes 1048608 | tf_op jit(solution)/shard_map/ppermute | solution.py:54
  83.0 0.9 slice.49
  84.0 0.0 collective-permute-start.17
  84.0 0.0 collective-permute-done.14.ahead
  84.0 0.9 slice.48
  84.8 3.2 %collective-permute-start.16 = (f32[1024,128]{1,0:T(8,128)}, f32[1024,128]{1,0:T(8,128)}, u32[]{:S(2)}, u32[]{:S(2)}) collective-permute-start(f32[1024,128]{1,0:T(8,128)} %slice.48), channel_id=1, source_target_pairs={{0,96},{1,25},{8,104},{9,1},{16,112},{17,9},{24,120},{25,17},{32,0... | collective-permute-start | bytes 1572872 | tf_op jit(solution)/shard_map/ppermute | solution.py:55
  88.1 6.2 %collective-permute-done.6.behind = f32[2048,128]{1,0:T(8,128)S(1)} collective-permute-done((f32[2048,128]{1,0:T(8,128)}, f32[2048,128]{1,0:T(8,128)S(1)}, u32[]{:S(2)}, u32[]{:S(2)}) %collective-permute-start.6) | collective-permute-done | bytes 1048608 | tf_op jit(solution)/shard_map/ppermute | solution.py:54
  94.3 0.9 slice.45
  95.2 1.9 %slice.44 = f32[1024,128]{1,0:T(8,128)} slice(f32[2048,128]{1,0:T(8,128)} %collective-permute-done.5.ahead), slice={[0:1024], [0:128]} | slice | bytes 1048576 | tf_op jit(solution)/shard_map/slice | solution.py:55
  97.1 3.2 %collective-permute-start.7 = (f32[1024,128]{1,0:T(8,128)}, f32[1024,128]{1,0:T(8,128)}, u32[]{:S(2)}, u32[]{:S(2)}) collective-permute-start(f32[1024,128]{1,0:T(8,128)} %slice.44), channel_id=1, source_target_pairs={{0,96},{1,25},{8,104},{9,1},{16,112},{17,9},{24,120},{25,17},{32,0... | collective-permute-start | bytes 1572872 | tf_op jit(solution)/shard_map/ppermute | solution.py:55
  100.3 14.9 %shard_map.68 = (f32[1024,128]{1,0:T(8,128)}, bf16[1024,1024]{1,0:T(8,128)(2,1)}, bf16[1024,1024]{1,0:T(8,128)(2,1)}) custom-call(s32[1]{0:T(128)} %bitcast.col_ref, f32[8,1024,128]{2,1,0:T(8,128)} %all-gather.2.cloned.1.call-done.rows_ref, f32[1024,1024]{1,0:T(8,128)} %inv_ref.1), custom_call_target="tpu_custom_call" | custom-call | flops 6442450944 | bytes 13631488 | tf_op jit(solution)/shard_map/pallas_call | solution.py:108
  115.3 14.6 %shard_map.69.rest_0_ = f32[1024,16,128]{2,1,0:T(8,128)} custom-call(s32[16]{0:T(128)} %fusion.place_ref, bf16[1024,1024]{1,0:T(8,128)(2,1)} %get-tuple-element.5.ghi, bf16[1024,1024]{1,0:T(8,128)(2,1)} %get-tuple-element.6.glo, f32[2048,128]{1,0:T(8,128)} %constant_dynamic-update-slice_fusion.5.held, f32[2048,128]{1,0:T(8,128)} %copy-done.1, ...), custom_call_target="tpu_custom_call" | custom-call | flops 6442450944 | bytes 16777216 | tf_op jit(solution)/shard_map/pallas_call | solution.py:181
  129.9 14.4 %shard_map.70 = f32[1024,16,128]{2,1,0:T(8,128)} custom-call(s32[16]{0:T(128)} %fusion.place_ref, bf16[1024,1024]{1,0:T(8,128)(2,1)} %get-tuple-element.5.ghi, bf16[1024,1024]{1,0:T(8,128)(2,1)} %get-tuple-element.6.glo, f32[2048,128]{1,0:T(8,128)} %constant_dynamic-update-slice_fusion.held, ...), custom_call_target="tpu_custom_call", output_to_operand_aliasing={{}: (9, {})} | custom-call | flops 6442450944 | bytes 16777216 | tf_op jit(solution)/shard_map/pallas_call | solution.py:181
  (24 shorter events, 0.1 us)
Async XLA Ops:
  7.2 67.5 %copy-start.3 = (s32[16]{0:T(128)S(1)}, s32[16]{0:T(128)}, u32[]{:S(2)}) copy-start(s32[16]{0:T(128)} %constant.63.clone) | copy-start | bytes 196
  7.2 67.5 %copy-start.4 = (s32[16]{0:T(128)S(1)}, s32[16]{0:T(128)}, u32[]{:S(2)}) copy-start(s32[16]{0:T(128)} %constant.62.clone) | copy-start | bytes 196
  7.2 93.1 %all-gather.2.cloned.1.call-start = ((), (), s32[]{:S(2)}) async-start(), calls=%async_computation | async-start | bytes 4718592 | tf_op jit(solution)/shard_map/all_gather | solution.py:223
  9.0 31.0 %collective-permute-start.9 = (f32[512,128]{1,0:T(8,128)S(1)}, f32[512,128]{1,0:T(8,128)S(1)}, u32[]{:S(2)}, u32[]{:S(2)}) collective-permute-start(f32[512,128]{1,0:T(8,128)S(1)} %get-tuple-element.12), channel_id=1, source_target_pairs={{0,0},{8,1},{16,2},{24,3},{32,4},{40,5},{48,6},{56,7},{1,8},{9,9},... | collective-permute-start | bytes 786440 | tf_op jit(solution)/shard_map/ppermute | solution.py:227
  15.7 35.4 %collective-permute-start = (f32[512,128]{1,0:T(8,128)S(1)}, f32[512,128]{1,0:T(8,128)S(1)}, u32[]{:S(2)}, u32[]{:S(2)}) collective-permute-start(f32[512,128]{1,0:T(8,128)S(1)} %get-tuple-element.13), channel_id=1, source_target_pairs={{0,0},{8,1},{16,2},{24,3},{32,4},{40,5},{48,6},{56,7},{1,8},{9,9},... | collective-permute-start | bytes 786440 | tf_op jit(solution)/shard_map/ppermute | solution.py:227
  40.0 15.8 %collective-permute-start.11 = (f32[512,128]{1,0:T(8,128)S(1)}, f32[512,128]{1,0:T(8,128)S(1)}, u32[]{:S(2)}, u32[]{:S(2)}) collective-permute-start(f32[512,128]{1,0:T(8,128)S(1)} %collective-permute-done.9), channel_id=1, source_target_pairs={{0,8},{1,33},{8,16},{9,41},{16,24},{17,49},{24,0},{25,57},{32,40},... | collective-permute-start | bytes 786440 | tf_op jit(solution)/shard_map/ppermute | solution.py:54
  40.0 15.9 %collective-permute-start.10 = (f32[512,128]{1,0:T(8,128)S(1)}, f32[512,128]{1,0:T(8,128)S(1)}, u32[]{:S(2)}, u32[]{:S(2)}) collective-permute-start(f32[512,128]{1,0:T(8,128)S(1)} %collective-permute-done.9), channel_id=1, source_target_pairs={{0,24},{1,97},{8,0},{9,105},{16,8},{17,113},{24,16},{25,121},{32,5... | collective-permute-start | bytes 786440 | tf_op jit(solution)/shard_map/ppermute | solution.py:53
  51.1 8.1 %collective-permute-start.2 = (f32[512,128]{1,0:T(8,128)S(1)}, f32[512,128]{1,0:T(8,128)S(1)}, u32[]{:S(2)}, u32[]{:S(2)}) collective-permute-start(f32[512,128]{1,0:T(8,128)S(1)} %collective-permute-done), channel_id=1, source_target_pairs={{0,8},{1,33},{8,16},{9,41},{16,24},{17,49},{24,0},{25,57},{32,40},... | collective-permute-start | bytes 786440 | tf_op jit(solution)/shard_map/ppermute | solution.py:54
  51.1 8.2 %collective-permute-start.1 = (f32[512,128]{1,0:T(8,128)S(1)}, f32[512,128]{1,0:T(8,128)S(1)}, u32[]{:S(2)}, u32[]{:S(2)}) collective-permute-start(f32[512,128]{1,0:T(8,128)S(1)} %collective-permute-done), channel_id=1, source_target_pairs={{0,24},{1,97},{8,0},{9,105},{16,8},{17,113},{24,16},{25,121},{32,5... | collective-permute-start | bytes 786440 | tf_op jit(solution)/shard_map/ppermute | solution.py:53
  55.8 10.3 %collective-permute-start.13 = (f32[256,128]{1,0:T(8,128)S(1)}, f32[256,128]{1,0:T(8,128)S(1)}, u32[]{:S(2)}, u32[]{:S(2)}) collective-permute-start(f32[256,128]{1,0:T(8,128)S(1)} %slice.47), channel_id=1, source_target_pairs={{0,8},{1,33},{8,16},{9,41},{16,24},{17,49},{24,0},{25,57},{32,40},... | collective-permute-start | bytes 393224 | tf_op jit(solution)/shard_map/ppermute | solution.py:56
  55.9 9.6 %collective-permute-start.12 = (f32[256,128]{1,0:T(8,128)S(1)}, f32[256,128]{1,0:T(8,128)S(1)}, u32[]{:S(2)}, u32[]{:S(2)}) collective-permute-start(f32[256,128]{1,0:T(8,128)S(1)} %slice.46), channel_id=1, source_target_pairs={{0,24},{1,97},{8,0},{9,105},{16,8},{17,113},{24,16},{25,121},{32,5... | collective-permute-start | bytes 393224 | tf_op jit(solution)/shard_map/ppermute | solution.py:55
  59.2 11.5 %collective-permute-start.4 = (f32[256,128]{1,0:T(8,128)S(1)}, f32[256,128]{1,0:T(8,128)S(1)}, u32[]{:S(2)}, u32[]{:S(2)}) collective-permute-start(f32[256,128]{1,0:T(8,128)S(1)} %slice.43), channel_id=1, source_target_pairs={{0,8},{1,33},{8,16},{9,41},{16,24},{17,49},{24,0},{25,57},{32,40},... | collective-permute-start | bytes 393224 | tf_op jit(solution)/shard_map/ppermute | solution.py:56
  59.4 10.7 %collective-permute-start.3 = (f32[256,128]{1,0:T(8,128)S(1)}, f32[256,128]{1,0:T(8,128)S(1)}, u32[]{:S(2)}, u32[]{:S(2)}) collective-permute-start(f32[256,128]{1,0:T(8,128)S(1)} %slice.42), channel_id=1, source_target_pairs={{0,24},{1,97},{8,0},{9,105},{16,8},{17,113},{24,16},{25,121},{32,5... | collective-permute-start | bytes 393224 | tf_op jit(solution)/shard_map/ppermute | solution.py:55
  66.8 16.2 %collective-permute-start.15 = (f32[2048,128]{1,0:T(8,128)}, f32[2048,128]{1,0:T(8,128)S(1)}, u32[]{:S(2)}, u32[]{:S(2)}) collective-permute-start(f32[2048,128]{1,0:T(8,128)} %constant_dynamic-update-slice_fusion.5.held), channel_id=1, source_target_pairs={{0,32},{1,9},{8,40},{9,17},{16,48},{17,25},{24,56},{25,1},{32,64},... | collective-permute-start | bytes 3145736 | tf_op jit(solution)/shard_map/ppermute | solution.py:54
  66.8 17.1 %collective-permute-start.14 = (f32[2048,128]{1,0:T(8,128)}, f32[2048,128]{1,0:T(8,128)S(1)}, u32[]{:S(2)}, u32[]{:S(2)}) collective-permute-start(f32[2048,128]{1,0:T(8,128)} %constant_dynamic-update-slice_fusion.5.held), channel_id=1, source_target_pairs={{0,96},{1,25},{8,104},{9,1},{16,112},{17,9},{24,120},{25,17},{32,0... | collective-permute-start | bytes 3145736 | tf_op jit(solution)/shard_map/ppermute | solution.py:53
  71.4 22.9 %collective-permute-start.6 = (f32[2048,128]{1,0:T(8,128)}, f32[2048,128]{1,0:T(8,128)S(1)}, u32[]{:S(2)}, u32[]{:S(2)}) collective-permute-start(f32[2048,128]{1,0:T(8,128)} %constant_dynamic-update-slice_fusion.held), channel_id=1, source_target_pairs={{0,32},{1,9},{8,40},{9,17},{16,48},{17,25},{24,56},{25,1},{32,64},... | collective-permute-start | bytes 3145736 | tf_op jit(solution)/shard_map/ppermute | solution.py:54
  71.4 23.8 %collective-permute-start.5 = (f32[2048,128]{1,0:T(8,128)}, f32[2048,128]{1,0:T(8,128)}, u32[]{:S(2)}, u32[]{:S(2)}) collective-permute-start(f32[2048,128]{1,0:T(8,128)} %constant_dynamic-update-slice_fusion.held), channel_id=1, source_target_pairs={{0,96},{1,25},{8,104},{9,1},{16,112},{17,9},{24,120},{25,17},{32,0... | collective-permute-start | bytes 3145736 | tf_op jit(solution)/shard_map/ppermute | solution.py:53
  83.0 32.2 %copy-start = (f32[2048,128]{1,0:T(8,128)}, f32[2048,128]{1,0:T(8,128)S(1)}, u32[]{:S(2)}) copy-start(f32[2048,128]{1,0:T(8,128)S(1)} %collective-permute-done.15.behind) | copy-start | bytes 3145732
  84.0 31.3 %collective-permute-start.17 = (f32[1024,128]{1,0:T(8,128)}, f32[1024,128]{1,0:T(8,128)}, u32[]{:S(2)}, u32[]{:S(2)}) collective-permute-start(f32[1024,128]{1,0:T(8,128)} %slice.49), channel_id=1, source_target_pairs={{0,32},{1,9},{8,40},{9,17},{16,48},{17,25},{24,56},{25,1},{32,64},... | collective-permute-start | bytes 1572872 | tf_op jit(solution)/shard_map/ppermute | solution.py:56
  84.0 31.3 %copy-start.1 = (f32[2048,128]{1,0:T(8,128)}, f32[2048,128]{1,0:T(8,128)S(1)}, u32[]{:S(2)}) copy-start(f32[2048,128]{1,0:T(8,128)S(1)} %collective-permute-done.14.ahead) | copy-start | bytes 3145732
  84.8 30.4 %collective-permute-start.16 = (f32[1024,128]{1,0:T(8,128)}, f32[1024,128]{1,0:T(8,128)}, u32[]{:S(2)}, u32[]{:S(2)}) collective-permute-start(f32[1024,128]{1,0:T(8,128)} %slice.48), channel_id=1, source_target_pairs={{0,96},{1,25},{8,104},{9,1},{16,112},{17,9},{24,120},{25,17},{32,0... | collective-permute-start | bytes 1572872 | tf_op jit(solution)/shard_map/ppermute | solution.py:55
  94.3 21.0 %copy-start.2 = (f32[2048,128]{1,0:T(8,128)}, f32[2048,128]{1,0:T(8,128)S(1)}, u32[]{:S(2)}) copy-start(f32[2048,128]{1,0:T(8,128)S(1)} %collective-permute-done.6.behind) | copy-start | bytes 3145732
  95.2 34.7 %collective-permute-start.8 = (f32[1024,128]{1,0:T(8,128)}, f32[1024,128]{1,0:T(8,128)}, u32[]{:S(2)}, u32[]{:S(2)}) collective-permute-start(f32[1024,128]{1,0:T(8,128)} %slice.45), channel_id=1, source_target_pairs={{0,32},{1,9},{8,40},{9,17},{16,48},{17,25},{24,56},{25,1},{32,64},... | collective-permute-start | bytes 1572872 | tf_op jit(solution)/shard_map/ppermute | solution.py:56
  97.1 32.8 %collective-permute-start.7 = (f32[1024,128]{1,0:T(8,128)}, f32[1024,128]{1,0:T(8,128)}, u32[]{:S(2)}, u32[]{:S(2)}) collective-permute-start(f32[1024,128]{1,0:T(8,128)} %slice.44), channel_id=1, source_target_pairs={{0,96},{1,25},{8,104},{9,1},{16,112},{17,9},{24,120},{25,17},{32,0... | collective-permute-start | bytes 1572872 | tf_op jit(solution)/shard_map/ppermute | solution.py:55
Sparse Core Ops, SparseCore 0:
  9.7 45.6 all-gather.1

commit v2 on v0

v2 whole, which is shorter than its diff:
```python
import functools

import jax
import jax.numpy as jnp
from jax import lax
from jax.experimental import pallas as pl
from jax.experimental.pallas import tpu as pltpu
from jax.sharding import PartitionSpec as P

BOTH = ("row", "col")
F32, BF16 = jnp.float32, jnp.bfloat16
LAST = (((1,), (1,)), ((), ()))
GF_FACTOR, GF_UPDATE = 4.0, 2.0
LIM = 44


def permutation(move):
    def index(x, y, z, core):
        return (y % 4 * 4 + z % 4) * 8 + x % 4 * 2 + core

    spots = [(x, y, z, core) for x in range(4) for y in range(4) for z in range(4) for core in (0, 1)]
    return [(index(*spot), index(*move(*spot))) for spot in spots]


def first_axis(step):
    return permutation(lambda x, y, z, core: (x, y + core * step, z + (1 - core) * step, core))


def second_axis(step):
    return permutation(lambda x, y, z, core: (x, y + (1 - core) * step, z + core * step, core))


def x_axis(step):
    return permutation(lambda x, y, z, core: (x + step, y, z, core))


OUTWARD = permutation(lambda x, y, z, core: (x - 1 + 2 * core, y, z, core))
SWAP = permutation(lambda x, y, z, core: (x, y, z, 1 - core))


def split(value):
    high = value.astype(BF16)
    return high, (value - high.astype(F32)).astype(BF16)


def dot3(left, right):
    dot = functools.partial(lax.dot_general, dimension_numbers=LAST, preferred_element_type=F32)
    return dot(left[0], right[0]) + (dot(left[0], right[1]) + dot(left[1], right[0]))


def call(kernel, out_shape, operands, in_specs, out_specs, scratch, megabytes, gigaflops, aliases=None):
    return pl.pallas_call(
        kernel,
        out_shape=out_shape,
        in_specs=in_specs,
        out_specs=out_specs,
        scratch_shapes=scratch,
        input_output_aliases=aliases or {},
        compiler_params=pltpu.CompilerParams(vmem_limit_bytes=megabytes * 2**20),
        cost_estimate=pl.CostEstimate(
            flops=int(gigaflops * 1e9), bytes_accessed=2**20, transcendentals=0
        ),
    )(*operands)


VMEM = pl.BlockSpec(memory_space=pltpu.VMEM)
ANY = pl.BlockSpec(memory_space=pl.ANY)


def place():
    row, col = lax.axis_index("row"), lax.axis_index("col")
    return col >> 1, col & 1, row >> 2, row & 3


def fetch_inverse(inv_hbm, inv_ref, sems, pieces):
    copies, wide = [], 256
    for j in range(inv_ref.shape[0] // wide):
        copies.append([])
        for at in range(pieces):
            tall = wide // pieces
            spot = (pl.ds(j * wide + at * tall, tall), pl.ds(0, (j + 1) * wide))
            copies[j].append(
                pltpu.make_async_copy(inv_hbm.at[spot], inv_ref.at[spot], sems.at[j, at])
            )
            copies[j][-1].start()
    return copies


def turn_kernel(rows_ref, out_ref):
    _, _, _, z = place()
    for at in range(8):
        turned = (at % 2) * 4 + at // 2 % 2 * 2 + at // 4
        out_ref[at] = rows_ref[jnp.where((z & 1) == 1, turned, at)]


def turn(rows):
    out = jax.ShapeDtypeStruct(rows.shape, F32)
    return call(turn_kernel, out, (rows,), [VMEM], VMEM, [], LIM, 0.5)


def slice_kernel(rows_ref, inv_ref, out_ref, bhi, blo):
    for k in range(rows_ref.shape[0]):
        high, low = split(rows_ref[k])
        bhi[:, k * 128 : (k + 1) * 128] = high
        blo[:, k * 128 : (k + 1) * 128] = low
    for j in range(inv_ref.shape[0] // 256):
        cols, upto = slice(j * 256, (j + 1) * 256), slice(0, (j + 1) * 256)
        out_ref[:, cols] = dot3((bhi[:, upto], blo[:, upto]), split(inv_ref[cols, upto]))


def factor_slice(rows, inv_factor):
    count, tall, _ = rows.shape
    order = inv_factor.shape[0]
    return call(
        slice_kernel,
        jax.ShapeDtypeStruct((tall, order), F32),
        (rows, inv_factor),
        [VMEM, VMEM],
        VMEM,
        [pltpu.VMEM((tall, order), BF16), pltpu.VMEM((tall, order), BF16)],
        LIM,
        0.5,
    )


def factor_kernel(*rest):
    x, core, _, _ = place()
    order = [(0, 0), (0, 1)] + [(step, side) for side in (0, 1) for step in (1, 3, 2)]
    pieces, rest = rest[:-11], rest[-11:]
    inv_hbm, own_ref, halves, line_ref, f_ref, bhi, blo, inv_ref, lhi, llo, sems = rest
    local, step = line_ref.shape[1], 256
    copies = []
    for ref in pieces:
        for piece in range(ref.shape[0] // local):
            at = len(copies)
            rows = pl.ds(piece * local, local)
            copies.append(pltpu.make_async_copy(ref.at[rows, :], line_ref.at[at], sems.at[0, at // 2, at % 2]))
            copies[-1].start()
    ready = fetch_inverse(inv_hbm, inv_ref, sems.at[1], 2)
    for at, copy in enumerate(copies):
        copy.wait()
        step_x, side = order[at]
        lane = pl.multiple_of((((x + step_x) & 3) * 2 + (core ^ side)) * 128, 128)
        high, low = split(line_ref[at])
        bhi[:, pl.ds(lane, 128)] = high
        blo[:, pl.ds(lane, 128)] = low
    for m in range(local // step):
        rows = slice(m * step, (m + 1) * step)
        for j, arriving in enumerate(ready):
            cols, upto = slice(j * 256, (j + 1) * 256), slice(0, (j + 1) * 256)
            if m == 0:
                for copy in arriving:
                    copy.wait()
                high, low = split(inv_ref[cols, upto])
                lhi[cols, upto] = high
                llo[cols, upto] = low
            value = dot3((bhi[rows, upto], blo[rows, upto]), (lhi[cols, upto], llo[cols, upto]))
            high, low = split(value)
            halves[0, rows, cols] = high
            halves[1, rows, cols] = low
            for side in range(2):
                f_ref[2 * j + side, rows, :] = value[:, side * 128 : (side + 1) * 128]
    own_ref[...] = f_ref[x * 2 + core]


def factor(pieces, inv_factor):
    local, order = pieces[0].shape[0], inv_factor.shape[0]
    return call(
        factor_kernel,
        (
            jax.ShapeDtypeStruct((local, 128), F32),
            jax.ShapeDtypeStruct((2, local, order), BF16),
        ),
        (*pieces, inv_factor),
        [ANY] * (len(pieces) + 1),
        (VMEM, VMEM),
        [
            pltpu.VMEM((order // 128, local, 128), F32),
            pltpu.VMEM((order // 128, local, 128), F32),
            pltpu.VMEM((local, order), BF16),
            pltpu.VMEM((local, order), BF16),
            pltpu.VMEM((order, order), F32),
            pltpu.VMEM((order, order), BF16),
            pltpu.VMEM((order, order), BF16),
            pltpu.SemaphoreType.DMA((2, 4, 2)),
        ],
        LIM,
        GF_FACTOR,
    )


NEAR, FAR = (0, 1), (3, 2)


def update_kernel(sources, f_ref, *rest):
    pieces, (a_ref, out_ref, buf, chi, clo, sems) = rest[:2], (rest[2], *rest[-5:])
    _, core, y, z = place()
    first, second = jnp.where(core == 0, z, y), jnp.where(core == 0, y, z)
    spot = []
    for move, steps in sources:
        p = (second + move) & 3
        for step in steps:
            q = (first + step) & 3
            other = (q >> 1) * 4 + (p >> 1) * 2 + (q & 1)
            spot.append(jnp.where(core == 0, (p >> 1) * 4 + q, other))
    local, step = buf.shape[0], 256
    group = pl.multiple_of(((second + sources[0][0]) & 1) * 8, 8)
    ins, outs = [], []
    for m in range(local // step):
        lines = pl.ds(m * step, step)
        here = a_ref.at[lines, pl.ds(group, 8), :]
        there = out_ref.at[lines, pl.ds(group, 8), :]
        ins.append(pltpu.make_async_copy(here, buf.at[lines], sems.at[0, m]))
        outs.append(pltpu.make_async_copy(buf.at[lines], there, sems.at[1, m]))
    for copy in ins:
        copy.start()
    for at, ref in enumerate(pieces):
        rows = slice(at * 256, (at + 1) * 256)
        high, low = split(ref[...])
        chi[rows, :] = high
        clo[rows, :] = low
    flat = buf.reshape(local * 8, 128)
    for m in range(local // step):
        lines = pl.ds(m * step, step)
        ins[m].wait()
        for n in range(2):
            cols = slice(n * 256, (n + 1) * 256)
            product = dot3((f_ref[0, lines, :], f_ref[1, lines, :]), (chi[cols, :], clo[cols, :]))
            for j in range(2):
                spots = pl.ds(m * step * 8 + spot[2 * n + j], step, 8)
                flat[spots, :] = flat[spots, :] - product[:, j * 128 : (j + 1) * 128]
        outs[m].start()
    for copy in outs:
        copy.wait()


def update(sources, f, pieces, source, so_far):
    _, local, order = f.shape
    operands = [f, *pieces, source]
    in_specs = [VMEM, VMEM, VMEM, ANY]
    aliases = {3: 0}
    if so_far is not source:
        aliases = {}
        if so_far is not None:
            aliases = {4: 0}
            operands.append(so_far)
            in_specs.append(ANY)
    return call(
        functools.partial(update_kernel, sources),
        jax.ShapeDtypeStruct(source.shape, F32),
        operands,
        in_specs,
        ANY,
        [
            pltpu.VMEM((local, 8, 128), F32),
            pltpu.VMEM((512, order), BF16),
            pltpu.VMEM((512, order), BF16),
            pltpu.SemaphoreType.DMA((2, local // 256)),
        ],
        LIM,
        GF_UPDATE,
        aliases,
    )


def pick_kernel(even_ref, odd_ref, out_ref):
    _, core, _, _ = place()

    @pl.when(core == 0)
    def _():
        out_ref[...] = even_ref[...]

    @pl.when(core == 1)
    def _():
        out_ref[...] = odd_ref[...]


def pick(even, odd):
    out = jax.ShapeDtypeStruct(even.shape, F32)
    return call(pick_kernel, out, (even, odd), [VMEM, VMEM], VMEM, [], LIM, 0.1)


def join_kernel(*refs):
    *parts, out_ref = refs
    rows = parts[0].shape[0]
    for at, part in enumerate(parts):
        out_ref[at * rows : (at + 1) * rows] = part[...]


def join(*parts):
    rows, cols = parts[0].shape
    return call(
        join_kernel,
        jax.ShapeDtypeStruct((len(parts) * rows, cols), F32),
        parts,
        [VMEM] * len(parts),
        VMEM,
        [],
        LIM,
        0.1,
    )


def per_device(trailing_block, panel_block, inv_factor):
    tiles, _, tile, cols_dev = panel_block.shape
    local = tiles * tile
    panel = panel_block.reshape(local, cols_dev)
    trailing = trailing_block.reshape(local, 16, 128)

    swapped = lax.ppermute(panel, BOTH, SWAP)
    line_ahead = lax.ppermute(panel, BOTH, x_axis(-1))
    line_behind = lax.ppermute(panel, BOTH, x_axis(1))
    mine = turn(panel.reshape(8, 128, cols_dev))
    halves = [list(range(8)), list(range(8, 16))]
    mine = lax.all_to_all(mine, "row", 0, 0, axis_index_groups=halves, tiled=True)
    mine, line_ahead, line_behind = lax.optimization_barrier((mine, line_ahead, line_behind))
    line_across = lax.ppermute(pick(line_ahead, line_behind), BOTH, OUTWARD)
    mine = lax.all_to_all(mine, "col", 0, 0, tiled=True)
    own = factor_slice(mine, inv_factor)

    ahead = lax.ppermute(own, BOTH, first_axis(-1))
    behind = lax.ppermute(own, BOTH, first_axis(1))
    across = lax.ppermute(own, BOTH, first_axis(2))

    line_ahead, line_behind, line_across, _ = lax.optimization_barrier(
        (line_ahead, line_behind, line_across, own)
    )
    others = join(line_ahead, line_behind, line_across)
    line = (panel, swapped, others, lax.ppermute(others, BOTH, SWAP))
    own_columns, f = factor(line, inv_factor)

    ahead, behind, across, f = lax.optimization_barrier((ahead, behind, across, f))
    near = join(own, ahead)
    near_ahead = lax.ppermute(near, BOTH, second_axis(-1))
    near_behind = lax.ppermute(near, BOTH, second_axis(1))
    far = join(behind, across)
    far_behind = lax.ppermute(far, BOTH, second_axis(1))
    far_ahead = lax.ppermute(far, BOTH, second_axis(-1))
    updated = update(((0, NEAR), (0, FAR)), f, (near, far), trailing, None)
    near_ahead, far_behind, updated = lax.optimization_barrier((near_ahead, far_behind, updated))
    near_across = lax.ppermute(near_ahead, BOTH, second_axis(-1))
    far_across = lax.ppermute(far_behind, BOTH, second_axis(1))

    updated = update(((1, NEAR), (3, FAR)), f, (near_ahead, far_behind), trailing, updated)
    updated = update(((1, FAR), (3, NEAR)), f, (far_ahead, near_behind), updated, updated)
    updated = update(((2, NEAR), (2, FAR)), f, (near_across, far_across), updated, updated)
    return updated.reshape(trailing_block.shape), own_columns.reshape(panel_block.shape)


def solution(mesh):
    return jax.shard_map(
        per_device,
        mesh=mesh,
        in_specs=(P(None, "row", None, None, "col", None), P(None, "row", None, "col"), P()),
        out_specs=(P(None, "row", None, None, "col", None), P(None, "row", None, "col")),
        check_vma=False,
    )
```

time: 268 us -> 101 us (0.38)
  waiting for transfers between devices: 144 us -> 12.7 us
  matrix products: 48.7 us -> 0 us
  Pallas kernels: 0 us -> 38.2 us
  other arithmetic: 31.4 us -> 0 us
  blocking collectives: 0 us -> 30.9 us
  local copies, waits for them, and re-layouts: 29.1 us -> 1.08 us
  starting transfers between devices: 0.08 us -> 16.3 us
  between operations: 14.1 us -> 0.92 us
    psum x1 -> x0, waiting for transfers between devices: 104 us -> none  [broadcast(): return lax.psum(block, axis)]
    dot_general x2 -> x0, matrix products: 48.7 us -> none  [contract_last(): lax.dot_general(left, right, (((1,), (1,)), ((), ())), precision=lax.Prec...]
    all_gather x1 -> x0, waiting for transfers between devices: 39.5 us -> none  [per_device(): shard_part = lax.all_gather(panel_block, 'col', axis=3, tiled=True)]
    pallas_call x0 -> x11, Pallas kernels: none -> 38.2 us  [call(): pl.pallas_call(kernel, out_shape=out_shape, in_specs=in_specs, out_specs=...]
    all_to_all x0 -> x2, blocking collectives: none -> 30.9 us  [the longest x1 15.7 us: per_device(): lax.all_to_all(mine, 'row', 0, 0, axis_index_groups=halves, tiled=True)]
    unnamed x1 -> x0, other arithmetic: 26.9 us -> none
    ppermute x0 -> x14, starting transfers between devices: none -> 16.3 us  [the longest x1 3.23 us: per_device(): near_across = lax.ppermute(near_ahead, BOTH, second_axis(-1))]
    reshape x1 -> x0, local copies, waits for them, and re-layouts: 13.5 us -> none  [per_device(): updated.reshape(trailing_block.shape)]
  transfers between devices with their start and end apart: 2 -> 14, of which waited for: 2 -> 6; matrix products, arithmetic and copies ran while one was open for 15% -> 0% of each run, Pallas kernels for 0% -> 31%
where the time goes in v2:
time: 101 us; the launch traced here: 100 us
  Pallas kernels  38.2 us (38%)
  blocking collectives  30.9 us (31%)
  starting transfers between devices  16.3 us (16%)
  waiting for transfers between devices  12.7 us (13%)
  local copies, waits for them, and re-layouts  1.08 us (1%)
    pallas_call x11, Pallas kernels, call(): pl.pallas_call(kernel, out_shape=out_shape, in_specs=in_specs, out_specs=...  38.2 us
    all_to_all x1, blocking collectives, per_device(): lax.all_to_all(mine, 'row', 0, 0, axis_index_groups=halves, tiled=True)  15.7 us
    all_to_all x1, blocking collectives, per_device(): mine = lax.all_to_all(mine, 'col', 0, 0, tiled=True)  15.2 us
    ppermute x1, waiting for transfers between devices, per_device(): behind = lax.ppermute(own, BOTH, first_axis(1))  4.09 us
    ppermute x1, waiting for transfers between devices, per_device(): near_across = lax.ppermute(near_ahead, BOTH, second_axis(-1))  3.74 us
    ppermute x1, waiting for transfers between devices, per_device(): far_behind = lax.ppermute(far, BOTH, second_axis(1))  3.63 us
    ppermute x1, starting transfers between devices, per_device(): near_across = lax.ppermute(near_ahead, BOTH, second_axis(-1))  3.23 us
    ppermute x1, starting transfers between devices, per_device(): near_ahead = lax.ppermute(near, BOTH, second_axis(-1))  2.62 us
  transfers between devices with their start and end apart: 14, of which 6 were waited for; matrix products, arithmetic and copies ran while one was open for 0% of the time, Pallas kernels for 31%

profile of v2, /device:TPU:6, one launch (start us, length us, event | category | flops | bytes accessed | tf_op | source)
XLA Modules:
  0.0 100.1 jit_solution(943477766439951336)
XLA Ops:
  0.6 0.0 copy-start
  0.6 0.5 collective-permute-start.1
  1.1 1.6 %collective-permute-start = (f32[1024,128]{1,0:T(8,128)}, f32[1024,128]{1,0:T(8,128)S(1)}, u32[]{:S(2)}, u32[]{:S(2)}) collective-permute-start(f32[1024,128]{1,0:T(8,128)} %bitcast.8), channel_id=1, source_target_pairs={{0,6},{1,7},{8,14},{9,15},{16,22},{17,23},{24,30},{25,31},{32,38},... | collective-permute-start | bytes 1572872 | tf_op jit(solution)/shard_map/ppermute | solution.py:311
  2.7 0.0 copy-start.1
  2.7 1.1 %copy-done.1 = f32[2,1,512,128]{3,2,1,0:T(8,128)S(1)} copy-done((f32[2,1,512,128]{3,2,1,0:T(8,128)S(1)}, f32[2,1,512,128]{3,2,1,0:T(8,128)}, u32[]{:S(2)}) %copy-start.1) | copy-done | bytes 524312
  3.8 0.0 copy-start.2
  3.9 15.7 %all_to_all.10 = f32[8,128,128]{2,1,0:T(8,128)S(1)} all-to-all(f32[8,128,128]{2,1,0:T(8,128)S(1)} %shard_map.50), channel_id=1, replica_groups={{0,8,16,24,32,40,48,56},{64,72,80,88,96,104,112,120},{1,9,17,25,33,41,4..., dimensions={0} | all-to-all | bytes 1048576 | tf_op jit(solution)/shard_map/all_to_all | solution.py:315
  19.6 0.0 collective-permute-done.1.odd_ref.refs_1_
  19.6 0.0 collective-permute-done.even_ref.refs_0_
  19.6 0.9 collective-permute-start.6
  20.5 15.2 %all_to_all.11.rows_ref = f32[8,128,128]{2,1,0:T(8,128)S(1)} all-to-all(f32[8,128,128]{2,1,0:T(8,128)S(1)} %all_to_all.10), channel_id=1, replica_groups=mesh['row'=16,'col'=8] {'col'}, dimensions={0} | all-to-all | bytes 1048576 | tf_op jit(solution)/shard_map/all_to_all | solution.py:318
  35.7 0.0 copy-done
  35.7 1.4 %shard_map.51.refs_0_ = f32[128,1024]{1,0:T(8,128)S(1)} custom-call(f32[8,128,128]{2,1,0:T(8,128)S(1)} %all_to_all.11.rows_ref, f32[1024,1024]{1,0:T(8,128)S(1)} %copy-done), custom_call_target="tpu_custom_call" | custom-call | flops 500000000 | bytes 1048576 | tf_op jit(solution)/shard_map/pallas_call | solution.py:52
  37.1 0.0 collective-permute-done.6.refs_2_
  37.1 0.1 shard_map.53.rest_2_
  37.3 0.1 collective-permute-start.7
  37.3 0.0 copy-done.2
  37.4 0.5 collective-permute-start.5
  37.8 0.9 collective-permute-start.4
  38.8 0.8 collective-permute-start.3
  39.5 2.5 %collective-permute-start.2 = (f32[128,1024]{1,0:T(8,128)S(1)}, f32[128,1024]{1,0:T(8,128)S(1)}, u32[]{:S(2)}, u32[]{:S(2)}) collective-permute-start(f32[128,1024]{1,0:T(8,128)S(1)} %shard_map.51.refs_0_), channel_id=1, source_target_pairs={{0,24},{1,97},{8,0},{9,105},{16,8},{17,113},{24,16},{25,121},{32,5... | collective-permute-start | bytes 1572872 | tf_op jit(solution)/shard_map/ppermute | solution.py:321
  42.0 0.0 collective-permute-done.5.rest_1_
  42.0 0.0 collective-permute-done.7.rest_3_
  42.0 8.0 %shard_map.54 = (f32[1024,128]{1,0:T(8,128)}, bf16[2,1024,1024]{2,1,0:T(8,128)(2,1)S(1)}) custom-call(f32[1024,128]{1,0:T(8,128)S(1)} %bitcast.11, f32[1024,128]{1,0:T(8,128)S(1)} %collective-permute-done.5.rest_1_, f32[3072,128]{1,0:T(8,128)S(1)} %shard_map.53.rest_2_, f32[3072,128]{1,0:T(8,128)S(1)} %collective-permute-done.7.rest_3_, f32[1024,1024]{1,0:T(8,128)} %rest_4_.1), custom_call_target="tpu_custom_call" | custom-call | flops 4000000000 | bytes 1048576 | tf_op jit(solution)/shard_map/pallas_call | solution.py:52
  50.0 0.0 collective-permute-done.4.refs_1_
  50.1 4.1 %collective-permute-done.3.refs_0_ = f32[128,1024]{1,0:T(8,128)S(1)} collective-permute-done((f32[128,1024]{1,0:T(8,128)S(1)}, f32[128,1024]{1,0:T(8,128)S(1)}, u32[]{:S(2)}, u32[]{:S(2)}) %collective-permute-start.3) | collective-permute-done | bytes 524320 | tf_op jit(solution)/shard_map/ppermute | solution.py:322
  54.2 0.0 collective-permute-done.2.refs_1_
  54.2 0.1 shard_map.55.rest_0_
  54.2 0.1 shard_map.56.rest_1_
  54.3 0.7 collective-permute-start.9
  55.0 2.6 %collective-permute-start.8 = (f32[256,1024]{1,0:T(8,128)S(1)}, f32[256,1024]{1,0:T(8,128)S(1)}, u32[]{:S(2)}, u32[]{:S(2)}) collective-permute-start(f32[256,1024]{1,0:T(8,128)S(1)} %shard_map.55.rest_0_), channel_id=1, source_target_pairs={{0,96},{1,25},{8,104},{9,1},{16,112},{17,9},{24,120},{25,17},{32,0... | collective-permute-start | bytes 3145736 | tf_op jit(solution)/shard_map/ppermute | solution.py:334
  57.6 0.8 collective-permute-start.12
  58.5 1.2 %collective-permute-start.13 = (f32[256,1024]{1,0:T(8,128)S(1)}, f32[256,1024]{1,0:T(8,128)S(1)}, u32[]{:S(2)}, u32[]{:S(2)}) collective-permute-start(f32[256,1024]{1,0:T(8,128)S(1)} %shard_map.55.rest_0_), channel_id=1, source_target_pairs={{0,32},{1,9},{8,40},{9,17},{16,48},{17,25},{24,56},{25,1},{32,64},... | collective-permute-start | bytes 3145736 | tf_op jit(solution)/shard_map/ppermute | solution.py:335
  59.6 7.1 %shard_map.57.rest_3_ = f32[1024,16,128]{2,1,0:T(8,128)} custom-call(bf16[2,1024,1024]{2,1,0:T(8,128)(2,1)S(1)} %get-tuple-element.24.f_ref, f32[256,1024]{1,0:T(8,128)S(1)} %shard_map.55.rest_0_, f32[256,1024]{1,0:T(8,128)S(1)} %shard_map.56.rest_1_, f32[1024,16,128]{2,1,0:T(8,128)} %bitcast.13), custom_call_target="tpu_custom_call" | custom-call | flops 2000000000 | bytes 1048576 | tf_op jit(solution)/shard_map/pallas_call | solution.py:52
  66.8 3.6 %collective-permute-done.9.rest_1_ = f32[256,1024]{1,0:T(8,128)S(1)} collective-permute-done((f32[256,1024]{1,0:T(8,128)S(1)}, f32[256,1024]{1,0:T(8,128)S(1)}, u32[]{:S(2)}, u32[]{:S(2)}) %collective-permute-start.9) | collective-permute-done | bytes 1048608 | tf_op jit(solution)/shard_map/ppermute | solution.py:337
  70.4 0.0 collective-permute-done.8.rest_0_
  70.4 3.2 %collective-permute-start.10 = (f32[256,1024]{1,0:T(8,128)S(1)}, f32[256,1024]{1,0:T(8,128)S(1)}, u32[]{:S(2)}, u32[]{:S(2)}) collective-permute-start(f32[256,1024]{1,0:T(8,128)S(1)} %collective-permute-done.8.rest_0_), channel_id=1, source_target_pairs={{0,96},{1,25},{8,104},{9,1},{16,112},{17,9},{24,120},{25,17},{32,0... | collective-permute-start | bytes 3145736 | tf_op jit(solution)/shard_map/ppermute | solution.py:341
  73.6 0.0 collective-permute-start.11
  73.6 7.1 %shard_map.58.rest_2_ = f32[1024,16,128]{2,1,0:T(8,128)} custom-call(bf16[2,1024,1024]{2,1,0:T(8,128)(2,1)S(1)} %get-tuple-element.24.f_ref, f32[256,1024]{1,0:T(8,128)S(1)} %collective-permute-done.8.rest_0_, f32[256,1024]{1,0:T(8,128)S(1)} %collective-permute-done.9.rest_1_, f32[1024,16,128]{2,1,0:T(8,128)} %bitcast.14, ...), custom_call_target="tpu_custom_call", output_to_operand_aliasing={{}: (4, {})} | custom-call | flops 2000000000 | bytes 1048576 | tf_op jit(solution)/shard_map/pallas_call | solution.py:52
  80.8 0.5 collective-permute-done.12.rest_0_
  81.2 0.4 collective-permute-done.13.rest_1_
  81.6 7.1 %shard_map.59.rest_2_ = f32[1024,16,128]{2,1,0:T(8,128)} custom-call(bf16[2,1024,1024]{2,1,0:T(8,128)(2,1)S(1)} %get-tuple-element.24.f_ref, f32[256,1024]{1,0:T(8,128)S(1)} %collective-permute-done.12.rest_0_, f32[256,1024]{1,0:T(8,128)S(1)} %collective-permute-done.13.rest_1_, f32[1024,16,128]{2,1,0:T(8,128)} %shard_map.58.rest_2_), custom_call_target="tpu_custom_call", output_to_operand_aliasing={{}: (3, {})} | custom-call | flops 2000000000 | bytes 1048576 | tf_op jit(solution)/shard_map/pallas_call | solution.py:52
  88.7 3.7 %collective-permute-done.10.rest_0_ = f32[256,1024]{1,0:T(8,128)S(1)} collective-permute-done((f32[256,1024]{1,0:T(8,128)S(1)}, f32[256,1024]{1,0:T(8,128)S(1)}, u32[]{:S(2)}, u32[]{:S(2)}) %collective-permute-start.10) | collective-permute-done | bytes 1048608 | tf_op jit(solution)/shard_map/ppermute | solution.py:341
  92.5 0.4 collective-permute-done.11.rest_1_
  92.9 7.1 %shard_map.60 = f32[1024,16,128]{2,1,0:T(8,128)} custom-call(bf16[2,1024,1024]{2,1,0:T(8,128)(2,1)S(1)} %get-tuple-element.24.f_ref, f32[256,1024]{1,0:T(8,128)S(1)} %collective-permute-done.10.rest_0_, f32[256,1024]{1,0:T(8,128)S(1)} %collective-permute-done.11.rest_1_, f32[1024,16,128]{2,1,0:T(8,128)} %shard_map.59.rest_2_), custom_call_target="tpu_custom_call", output_to_operand_aliasing={{}: (3, {})} | custom-call | flops 2000000000 | bytes 1048576 | tf_op jit(solution)/shard_map/pallas_call | solution.py:52
  (2 shorter events, 0.1 us)
Async XLA Ops:
  0.6 35.1 %copy-start = (f32[1024,1024]{1,0:T(8,128)S(1)}, f32[1024,1024]{1,0:T(8,128)}, u32[]{:S(2)}) copy-start(f32[1024,1024]{1,0:T(8,128)} %rest_4_.1) | copy-start | bytes 12582916
  0.6 18.9 %collective-permute-start.1 = (f32[1024,128]{1,0:T(8,128)}, f32[1024,128]{1,0:T(8,128)S(1)}, u32[]{:S(2)}, u32[]{:S(2)}) collective-permute-start(f32[1024,128]{1,0:T(8,128)} %bitcast.7), channel_id=1, source_target_pairs={{0,2},{1,3},{8,10},{9,11},{16,18},{17,19},{24,26},{25,27},{32,34},... | collective-permute-start | bytes 1572872 | tf_op jit(solution)/shard_map/ppermute | solution.py:312
  1.1 18.5 %collective-permute-start = (f32[1024,128]{1,0:T(8,128)}, f32[1024,128]{1,0:T(8,128)S(1)}, u32[]{:S(2)}, u32[]{:S(2)}) collective-permute-start(f32[1024,128]{1,0:T(8,128)} %bitcast.8), channel_id=1, source_target_pairs={{0,6},{1,7},{8,14},{9,15},{16,22},{17,23},{24,30},{25,31},{32,38},... | collective-permute-start | bytes 1572872 | tf_op jit(solution)/shard_map/ppermute | solution.py:311
  2.7 1.1 %copy-start.1 = (f32[2,1,512,128]{3,2,1,0:T(8,128)S(1)}, f32[2,1,512,128]{3,2,1,0:T(8,128)}, u32[]{:S(2)}) copy-start(f32[2,1,512,128]{3,2,1,0:T(8,128)} %param.4) | copy-start | bytes 1572868
  3.8 33.5 %copy-start.2 = (f32[2,1,512,128]{3,2,1,0:T(8,128)S(1)}, f32[2,1,512,128]{3,2,1,0:T(8,128)}, u32[]{:S(2)}) copy-start(f32[2,1,512,128]{3,2,1,0:T(8,128)} %param.4) | copy-start | bytes 1572868
  19.6 17.5 %collective-permute-start.6 = (f32[1024,128]{1,0:T(8,128)S(1)}, f32[1024,128]{1,0:T(8,128)S(1)}, u32[]{:S(2)}, u32[]{:S(2)}) collective-permute-start(f32[1024,128]{1,0:T(8,128)S(1)} %shard_map.52), channel_id=1, source_target_pairs={{0,6},{1,3},{8,14},{9,11},{16,22},{17,19},{24,30},{25,27},{32,38},... | collective-permute-start | bytes 1572872 | tf_op jit(solution)/shard_map/ppermute | solution.py:317
  37.3 4.8 %collective-permute-start.7 = (f32[3072,128]{1,0:T(8,128)S(1)}, f32[3072,128]{1,0:T(8,128)S(1)}, u32[]{:S(2)}, u32[]{:S(2)}) collective-permute-start(f32[3072,128]{1,0:T(8,128)S(1)} %shard_map.53.rest_2_), channel_id=1, source_target_pairs={{0,1},{1,0},{8,9},{9,8},{16,17},{17,16},{24,25},{25,24},{32,33},{3... | collective-permute-start | bytes 4718600 | tf_op jit(solution)/shard_map/ppermute | solution.py:329
  37.4 4.6 %collective-permute-start.5 = (f32[1024,128]{1,0:T(8,128)S(1)}, f32[1024,128]{1,0:T(8,128)S(1)}, u32[]{:S(2)}, u32[]{:S(2)}) collective-permute-start(f32[1024,128]{1,0:T(8,128)S(1)} %bitcast.10), channel_id=1, source_target_pairs={{0,1},{1,0},{8,9},{9,8},{16,17},{17,16},{24,25},{25,24},{32,33},{3... | collective-permute-start | bytes 1572872 | tf_op jit(solution)/shard_map/ppermute | solution.py:310
  37.8 12.2 %collective-permute-start.4 = (f32[128,1024]{1,0:T(8,128)S(1)}, f32[128,1024]{1,0:T(8,128)S(1)}, u32[]{:S(2)}, u32[]{:S(2)}) collective-permute-start(f32[128,1024]{1,0:T(8,128)S(1)} %shard_map.51.refs_0_), channel_id=1, source_target_pairs={{0,16},{1,65},{8,24},{9,73},{16,0},{17,81},{24,8},{25,89},{32,48},... | collective-permute-start | bytes 1572872 | tf_op jit(solution)/shard_map/ppermute | solution.py:323
  38.8 15.4 %collective-permute-start.3 = (f32[128,1024]{1,0:T(8,128)S(1)}, f32[128,1024]{1,0:T(8,128)S(1)}, u32[]{:S(2)}, u32[]{:S(2)}) collective-permute-start(f32[128,1024]{1,0:T(8,128)S(1)} %shard_map.51.refs_0_), channel_id=1, source_target_pairs={{0,8},{1,33},{8,16},{9,41},{16,24},{17,49},{24,0},{25,57},{32,40},... | collective-permute-start | bytes 1572872 | tf_op jit(solution)/shard_map/ppermute | solution.py:322
  39.5 14.6 %collective-permute-start.2 = (f32[128,1024]{1,0:T(8,128)S(1)}, f32[128,1024]{1,0:T(8,128)S(1)}, u32[]{:S(2)}, u32[]{:S(2)}) collective-permute-start(f32[128,1024]{1,0:T(8,128)S(1)} %shard_map.51.refs_0_), channel_id=1, source_target_pairs={{0,24},{1,97},{8,0},{9,105},{16,8},{17,113},{24,16},{25,121},{32,5... | collective-permute-start | bytes 1572872 | tf_op jit(solution)/shard_map/ppermute | solution.py:321
  54.3 16.1 %collective-permute-start.9 = (f32[256,1024]{1,0:T(8,128)S(1)}, f32[256,1024]{1,0:T(8,128)S(1)}, u32[]{:S(2)}, u32[]{:S(2)}) collective-permute-start(f32[256,1024]{1,0:T(8,128)S(1)} %shard_map.56.rest_1_), channel_id=1, source_target_pairs={{0,32},{1,9},{8,40},{9,17},{16,48},{17,25},{24,56},{25,1},{32,64},... | collective-permute-start | bytes 3145736 | tf_op jit(solution)/shard_map/ppermute | solution.py:337
  55.0 15.4 %collective-permute-start.8 = (f32[256,1024]{1,0:T(8,128)S(1)}, f32[256,1024]{1,0:T(8,128)S(1)}, u32[]{:S(2)}, u32[]{:S(2)}) collective-permute-start(f32[256,1024]{1,0:T(8,128)S(1)} %shard_map.55.rest_0_), channel_id=1, source_target_pairs={{0,96},{1,25},{8,104},{9,1},{16,112},{17,9},{24,120},{25,17},{32,0... | collective-permute-start | bytes 3145736 | tf_op jit(solution)/shard_map/ppermute | solution.py:334
  57.6 23.6 %collective-permute-start.12 = (f32[256,1024]{1,0:T(8,128)S(1)}, f32[256,1024]{1,0:T(8,128)S(1)}, u32[]{:S(2)}, u32[]{:S(2)}) collective-permute-start(f32[256,1024]{1,0:T(8,128)S(1)} %shard_map.56.rest_1_), channel_id=1, source_target_pairs={{0,96},{1,25},{8,104},{9,1},{16,112},{17,9},{24,120},{25,17},{32,0... | collective-permute-start | bytes 3145736 | tf_op jit(solution)/shard_map/ppermute | solution.py:338
  58.5 23.2 %collective-permute-start.13 = (f32[256,1024]{1,0:T(8,128)S(1)}, f32[256,1024]{1,0:T(8,128)S(1)}, u32[]{:S(2)}, u32[]{:S(2)}) collective-permute-start(f32[256,1024]{1,0:T(8,128)S(1)} %shard_map.55.rest_0_), channel_id=1, source_target_pairs={{0,32},{1,9},{8,40},{9,17},{16,48},{17,25},{24,56},{25,1},{32,64},... | collective-permute-start | bytes 3145736 | tf_op jit(solution)/shard_map/ppermute | solution.py:335
  70.4 22.1 %collective-permute-start.10 = (f32[256,1024]{1,0:T(8,128)S(1)}, f32[256,1024]{1,0:T(8,128)S(1)}, u32[]{:S(2)}, u32[]{:S(2)}) collective-permute-start(f32[256,1024]{1,0:T(8,128)S(1)} %collective-permute-done.8.rest_0_), channel_id=1, source_target_pairs={{0,96},{1,25},{8,104},{9,1},{16,112},{17,9},{24,120},{25,17},{32,0... | collective-permute-start | bytes 3145736 | tf_op jit(solution)/shard_map/ppermute | solution.py:341
  73.6 19.2 %collective-permute-start.11 = (f32[256,1024]{1,0:T(8,128)S(1)}, f32[256,1024]{1,0:T(8,128)S(1)}, u32[]{:S(2)}, u32[]{:S(2)}) collective-permute-start(f32[256,1024]{1,0:T(8,128)S(1)} %collective-permute-done.9.rest_1_), channel_id=1, source_target_pairs={{0,32},{1,9},{8,40},{9,17},{16,48},{17,25},{24,56},{25,1},{32,64},... | collective-permute-start | bytes 3145736 | tf_op jit(solution)/shard_map/ppermute | solution.py:342

commit v3 on v2

--- a/solution.py
+++ b/solution.py
@@ -11,7 +11,7 @@
 F32, BF16 = jnp.float32, jnp.bfloat16
 LAST = (((1,), (1,)), ((), ()))
 GF_FACTOR, GF_UPDATE = 4.0, 2.0
-LIM = 44
+LIM = 40
 
 
 def permutation(move):
@@ -192,8 +192,7 @@
 NEAR, FAR = (0, 1), (3, 2)
 
 
-def update_kernel(sources, f_ref, *rest):
-    pieces, (a_ref, out_ref, buf, chi, clo, sems) = rest[:2], (rest[2], *rest[-5:])
+def sub_rows(sources):
     _, core, y, z = place()
     first, second = jnp.where(core == 0, z, y), jnp.where(core == 0, y, z)
     spot = []
@@ -203,63 +202,95 @@
             q = (first + step) & 3
             other = (q >> 1) * 4 + (p >> 1) * 2 + (q & 1)
             spot.append(jnp.where(core == 0, (p >> 1) * 4 + q, other))
-    local, step = buf.shape[0], 256
     group = pl.multiple_of(((second + sources[0][0]) & 1) * 8, 8)
-    ins, outs = [], []
-    for m in range(local // step):
-        lines = pl.ds(m * step, step)
-        here = a_ref.at[lines, pl.ds(group, 8), :]
-        there = out_ref.at[lines, pl.ds(group, 8), :]
-        ins.append(pltpu.make_async_copy(here, buf.at[lines], sems.at[0, m]))
-        outs.append(pltpu.make_async_copy(buf.at[lines], there, sems.at[1, m]))
-    for copy in ins:
-        copy.start()
+    return group, spot
+
+
+def split_pieces(pieces, chi, clo):
     for at, ref in enumerate(pieces):
         rows = slice(at * 256, (at + 1) * 256)
         high, low = split(ref[...])
         chi[rows, :] = high
         clo[rows, :] = low
-    flat = buf.reshape(local * 8, 128)
-    for m in range(local // step):
-        lines = pl.ds(m * step, step)
-        ins[m].wait()
-        for n in range(2):
-            cols = slice(n * 256, (n + 1) * 256)
-            product = dot3((f_ref[0, lines, :], f_ref[1, lines, :]), (chi[cols, :], clo[cols, :]))
-            for j in range(2):
-                spots = pl.ds(m * step * 8 + spot[2 * n + j], step, 8)
-                flat[spots, :] = flat[spots, :] - product[:, j * 128 : (j + 1) * 128]
-        outs[m].start()
-    for copy in outs:
+
+
+def subtract(m, spot, f_ref, chi, clo, buf):
+    step = 256
+    lines = pl.ds(m * step, step)
+    flat = buf.reshape(buf.shape[0] * 8, 128)
+    for n in range(2):
+        cols = slice(n * 256, (n + 1) * 256)
+        product = dot3((f_ref[0, lines, :], f_ref[1, lines, :]), (chi[cols, :], clo[cols, :]))
+        for j in range(2):
+            spots = pl.ds(m * step * 8 + spot[2 * n + j], step, 8)
+            flat[spots, :] = flat[spots, :] - product[:, j * 128 : (j + 1) * 128]
+
+
+def open_kernel(sources, f_ref, near, far, a_ref, held, chi, clo, sems):
+    group, spot = sub_rows(sources)
+    copies = []
+    for m in range(held.shape[0] // 256):
+        lines = pl.ds(m * 256, 256)
+        here = a_ref.at[lines, pl.ds(group, 8), :]
+        copies.append(pltpu.make_async_copy(here, held.at[lines], sems.at[m]))
+        copies[-1].start()
+    split_pieces((near, far), chi, clo)
+    for m, copy in enumerate(copies):
         copy.wait()
-
-
-def update(sources, f, pieces, source, so_far):
+        subtract(m, spot, f_ref, chi, clo, held)
+
+
+def close_kernel(sources, f_ref, near, far, held, *rest):
+    out_ref, buf, chi, clo, sems = rest[-5:]
+    group, spot = sub_rows(sources)
+    split_pieces((near, far), chi, clo)
+    copies = []
+    for m in range(buf.shape[0] // 256):
+        lines = pl.ds(m * 256, 256)
+        buf[lines] = held[lines]
+        subtract(m, spot, f_ref, chi, clo, buf)
+        there = out_ref.at[lines, pl.ds(group, 8), :]
+        copies.append(pltpu.make_async_copy(buf.at[lines], there, sems.at[m]))
+        copies[-1].start()
+    for copy in copies:
+        copy.wait()
+
+
+def update_scratch(local, order):
+    return [
+        pltpu.VMEM((512, order), BF16),
+        pltpu.VMEM((512, order), BF16),
+        pltpu.SemaphoreType.DMA((local // 256,)),
+    ]
+
+
+def open_group(sources, f, pieces, trailing):
     _, local, order = f.shape
-    operands = [f, *pieces, source]
-    in_specs = [VMEM, VMEM, VMEM, ANY]
-    aliases = {3: 0}
-    if so_far is not source:
-        aliases = {}
-        if so_far is not None:
-            aliases = {4: 0}
-            operands.append(so_far)
-            in_specs.append(ANY)
-    return call(
-        functools.partial(update_kernel, sources),
-        jax.ShapeDtypeStruct(source.shape, F32),
-        operands,
-        in_specs,
+    return call(
+        functools.partial(open_kernel, sources),
+        jax.ShapeDtypeStruct((local, 8, 128), F32),
+        (f, *pieces, trailing),
+        [VMEM, VMEM, VMEM, ANY],
+        VMEM,
+        update_scratch(local, order),
+        LIM,
+        GF_UPDATE,
+    )
+
+
+def close_group(sources, f, pieces, held, shape, so_far):
+    _, local, order = f.shape
+    after = () if so_far is None else (so_far,)
+    return call(
+        functools.partial(close_kernel, sources),
+        jax.ShapeDtypeStruct(shape, F32),
+        (f, *pieces, held, *after),
+        [VMEM] * 4 + [ANY] * len(after),
         ANY,
-        [
-            pltpu.VMEM((local, 8, 128), F32),
-            pltpu.VMEM((512, order), BF16),
-            pltpu.VMEM((512, order), BF16),
-            pltpu.SemaphoreType.DMA((2, local // 256)),
-        ],
+        [pltpu.VMEM((local, 8, 128), F32), *update_scratch(local, order)],
         LIM,
         GF_UPDATE,
-        aliases,
+        {4: 0} if after else {},
     )
 
 
@@ -336,14 +367,16 @@
     far = join(behind, across)
     far_behind = lax.ppermute(far, BOTH, second_axis(1))
     far_ahead = lax.ppermute(far, BOTH, second_axis(-1))
-    updated = update(((0, NEAR), (0, FAR)), f, (near, far), trailing, None)
-    near_ahead, far_behind, updated = lax.optimization_barrier((near_ahead, far_behind, updated))
+    held = open_group(((0, NEAR), (0, FAR)), f, (near, far), trailing)
+    near_ahead, far_behind, held = lax.optimization_barrier((near_ahead, far_behind, held))
     near_across = lax.ppermute(near_ahead, BOTH, second_axis(-1))
     far_across = lax.ppermute(far_behind, BOTH, second_axis(1))
 
-    updated = update(((1, NEAR), (3, FAR)), f, (near_ahead, far_behind), trailing, updated)
-    updated = update(((1, FAR), (3, NEAR)), f, (far_ahead, near_behind), updated, updated)
-    updated = update(((2, NEAR), (2, FAR)), f, (near_across, far_across), updated, updated)
+    beside = open_group(((1, NEAR), (3, FAR)), f, (near_ahead, far_behind), trailing)
+    pieces, shape = (far_ahead, near_behind), trailing.shape
+    updated = close_group(((1, FAR), (3, NEAR)), f, pieces, beside, shape, None)
+    pieces = (near_across, far_across)
+    updated = close_group(((2, NEAR), (2, FAR)), f, pieces, held, shape, updated)
     return updated.reshape(trailing_block.shape), own_columns.reshape(panel_block.shape)
 
 

time: 101 us -> 98.7 us (0.977)
  Pallas kernels: 38.2 us -> 33 us
  waiting for transfers between devices: 12.7 us -> 16.2 us
    pallas_call x11, Pallas kernels: 38.2 us -> 33 us  [call(): pl.pallas_call(kernel, out_shape=out_shape, in_specs=in_specs, out_specs=...]
    ppermute x1, waiting for transfers between devices: 3.74 us -> 5.48 us  [per_device(): near_across = lax.ppermute(near_ahead, BOTH, second_axis(-1))]
    ppermute x1, waiting for transfers between devices: 0.48 us -> 1.5 us  [per_device(): far_ahead = lax.ppermute(far, BOTH, second_axis(-1))]
  transfers between devices with their start and end apart: 14 -> 14, of which waited for: 6 -> 6; matrix products, arithmetic and copies ran while one was open for 0% -> 0% of each run, Pallas kernels for 31% -> 28%
where the time goes in v3:
time: 98.7 us; the launch traced here: 98.3 us
  Pallas kernels  33 us (33%)
  blocking collectives  30.8 us (31%)
  starting transfers between devices  16.3 us (17%)
  waiting for transfers between devices  16.2 us (16%)
  local copies, waits for them, and re-layouts  1.08 us (1%)
    pallas_call x11, Pallas kernels, call(): pl.pallas_call(kernel, out_shape=out_shape, in_specs=in_specs, out_specs=...  33 us
    all_to_all x1, blocking collectives, per_device(): lax.all_to_all(mine, 'row', 0, 0, axis_index_groups=halves, tiled=True)  15.6 us
    all_to_all x1, blocking collectives, per_device(): mine = lax.all_to_all(mine, 'col', 0, 0, tiled=True)  15.2 us
    ppermute x1, waiting for transfers between devices, per_device(): near_across = lax.ppermute(near_ahead, BOTH, second_axis(-1))  5.48 us
    ppermute x1, waiting for transfers between devices, per_device(): far_behind = lax.ppermute(far, BOTH, second_axis(1))  4.63 us
    ppermute x1, waiting for transfers between devices, per_device(): behind = lax.ppermute(own, BOTH, first_axis(1))  3.87 us
    ppermute x1, starting transfers between devices, per_device(): near_across = lax.ppermute(near_ahead, BOTH, second_axis(-1))  3.23 us
    ppermute x1, starting transfers between devices, per_device(): near_ahead = lax.ppermute(near, BOTH, second_axis(-1))  2.62 us
  transfers between devices with their start and end apart: 14, of which 6 were waited for; matrix products, arithmetic and copies ran while one was open for 0% of the time, Pallas kernels for 28%

profile of v3, /device:TPU:6, one launch (start us, length us, event | category | flops | bytes accessed | tf_op | source)
XLA Modules:
  0.0 98.3 jit_solution(13852256671909137105)
XLA Ops:
  0.6 0.0 copy-start
  0.6 0.5 collective-permute-start.1
  1.1 1.6 %collective-permute-start = (f32[1024,128]{1,0:T(8,128)}, f32[1024,128]{1,0:T(8,128)S(1)}, u32[]{:S(2)}, u32[]{:S(2)}) collective-permute-start(f32[1024,128]{1,0:T(8,128)} %bitcast.8), channel_id=1, source_target_pairs={{0,6},{1,7},{8,14},{9,15},{16,22},{17,23},{24,30},{25,31},{32,38},... | collective-permute-start | bytes 1572872 | tf_op jit(solution)/shard_map/ppermute | solution.py:342
  2.7 0.0 copy-start.1
  2.7 1.1 %copy-done.1 = f32[2,1,512,128]{3,2,1,0:T(8,128)S(1)} copy-done((f32[2,1,512,128]{3,2,1,0:T(8,128)S(1)}, f32[2,1,512,128]{3,2,1,0:T(8,128)}, u32[]{:S(2)}) %copy-start.1) | copy-done | bytes 524312
  3.8 15.6 %all_to_all.10 = f32[8,128,128]{2,1,0:T(8,128)S(1)} all-to-all(f32[8,128,128]{2,1,0:T(8,128)S(1)} %shard_map.50), channel_id=1, replica_groups={{0,8,16,24,32,40,48,56},{64,72,80,88,96,104,112,120},{1,9,17,25,33,41,4..., dimensions={0} | all-to-all | bytes 1048576 | tf_op jit(solution)/shard_map/all_to_all | solution.py:346
  19.4 0.0 collective-permute-done.1.odd_ref.refs_1_
  19.4 0.0 collective-permute-done.even_ref.refs_0_
  19.5 0.9 collective-permute-start.6
  20.4 15.2 %all_to_all.11.rows_ref = f32[8,128,128]{2,1,0:T(8,128)S(1)} all-to-all(f32[8,128,128]{2,1,0:T(8,128)S(1)} %all_to_all.10), channel_id=1, replica_groups=mesh['row'=16,'col'=8] {'col'}, dimensions={0} | all-to-all | bytes 1048576 | tf_op jit(solution)/shard_map/all_to_all | solution.py:349
  35.6 0.0 copy-done
  35.6 0.0 copy-start.2
  35.6 1.4 %shard_map.51.refs_0_ = f32[128,1024]{1,0:T(8,128)S(1)} custom-call(f32[8,128,128]{2,1,0:T(8,128)S(1)} %all_to_all.11.rows_ref, f32[1024,1024]{1,0:T(8,128)S(1)} %copy-done), custom_call_target="tpu_custom_call" | custom-call | flops 500000000 | bytes 1048576 | tf_op jit(solution)/shard_map/pallas_call | solution.py:52
  37.0 0.0 collective-permute-done.6.refs_2_
  37.0 0.1 shard_map.53.rest_2_
  37.1 0.1 collective-permute-start.7
  37.2 0.0 copy-done.2
  37.2 0.5 collective-permute-start.5
  37.7 0.9 collective-permute-start.4
  38.6 0.8 collective-permute-start.3
  39.4 2.5 %collective-permute-start.2 = (f32[128,1024]{1,0:T(8,128)S(1)}, f32[128,1024]{1,0:T(8,128)S(1)}, u32[]{:S(2)}, u32[]{:S(2)}) collective-permute-start(f32[128,1024]{1,0:T(8,128)S(1)} %shard_map.51.refs_0_), channel_id=1, source_target_pairs={{0,24},{1,97},{8,0},{9,105},{16,8},{17,113},{24,16},{25,121},{32,5... | collective-permute-start | bytes 1572872 | tf_op jit(solution)/shard_map/ppermute | solution.py:352
  41.9 0.0 collective-permute-done.5.rest_1_
  41.9 0.0 collective-permute-done.7.rest_3_
  41.9 8.3 %shard_map.54 = (f32[1024,128]{1,0:T(8,128)}, bf16[2,1024,1024]{2,1,0:T(8,128)(2,1)S(1)}) custom-call(f32[1024,128]{1,0:T(8,128)S(1)} %bitcast.11, f32[1024,128]{1,0:T(8,128)S(1)} %collective-permute-done.5.rest_1_, f32[3072,128]{1,0:T(8,128)S(1)} %shard_map.53.rest_2_, f32[3072,128]{1,0:T(8,128)S(1)} %collective-permute-done.7.rest_3_, f32[1024,1024]{1,0:T(8,128)S(1)} %copy-done), custom_call_target="tpu_custom_call" | custom-call | flops 4000000000 | bytes 1048576 | tf_op jit(solution)/shard_map/pallas_call | solution.py:52
  50.1 0.0 collective-permute-done.4.refs_1_
  50.1 3.9 %collective-permute-done.3.refs_0_ = f32[128,1024]{1,0:T(8,128)S(1)} collective-permute-done((f32[128,1024]{1,0:T(8,128)S(1)}, f32[128,1024]{1,0:T(8,128)S(1)}, u32[]{:S(2)}, u32[]{:S(2)}) %collective-permute-start.3) | collective-permute-done | bytes 524320 | tf_op jit(solution)/shard_map/ppermute | solution.py:353
  54.0 0.0 collective-permute-done.2.refs_1_
  54.0 0.1 shard_map.55.near
  54.1 0.1 shard_map.56.far
  54.2 0.7 collective-permute-start.9
  54.9 2.6 %collective-permute-start.8 = (f32[256,1024]{1,0:T(8,128)S(1)}, f32[256,1024]{1,0:T(8,128)S(1)}, u32[]{:S(2)}, u32[]{:S(2)}) collective-permute-start(f32[256,1024]{1,0:T(8,128)S(1)} %shard_map.55.near), channel_id=1, source_target_pairs={{0,96},{1,25},{8,104},{9,1},{16,112},{17,9},{24,120},{25,17},{32,0... | collective-permute-start | bytes 3145736 | tf_op jit(solution)/shard_map/ppermute | solution.py:365
  57.5 0.8 collective-permute-start.12
  58.3 1.2 %collective-permute-start.13 = (f32[256,1024]{1,0:T(8,128)S(1)}, f32[256,1024]{1,0:T(8,128)S(1)}, u32[]{:S(2)}, u32[]{:S(2)}) collective-permute-start(f32[256,1024]{1,0:T(8,128)S(1)} %shard_map.55.near), channel_id=1, source_target_pairs={{0,32},{1,9},{8,40},{9,17},{16,48},{17,25},{24,56},{25,1},{32,64},... | collective-permute-start | bytes 3145736 | tf_op jit(solution)/shard_map/ppermute | solution.py:366
  59.5 6.1 %shard_map.57.held = f32[1024,8,128]{2,1,0:T(8,128)S(1)} custom-call(bf16[2,1024,1024]{2,1,0:T(8,128)(2,1)S(1)} %get-tuple-element.24.f_ref, f32[256,1024]{1,0:T(8,128)S(1)} %shard_map.55.near, f32[256,1024]{1,0:T(8,128)S(1)} %shard_map.56.far, f32[1024,16,128]{2,1,0:T(8,128)} %bitcast.12), custom_call_target="tpu_custom_call" | custom-call | flops 2000000000 | bytes 1048576 | tf_op jit(solution)/shard_map/pallas_call | solution.py:52
  65.6 4.6 %collective-permute-done.9.far = f32[256,1024]{1,0:T(8,128)S(1)} collective-permute-done((f32[256,1024]{1,0:T(8,128)S(1)}, f32[256,1024]{1,0:T(8,128)S(1)}, u32[]{:S(2)}, u32[]{:S(2)}) %collective-permute-start.9) | collective-permute-done | bytes 1048608 | tf_op jit(solution)/shard_map/ppermute | solution.py:368
  70.2 0.0 collective-permute-done.8.near
  70.3 3.2 %collective-permute-start.10 = (f32[256,1024]{1,0:T(8,128)S(1)}, f32[256,1024]{1,0:T(8,128)S(1)}, u32[]{:S(2)}, u32[]{:S(2)}) collective-permute-start(f32[256,1024]{1,0:T(8,128)S(1)} %collective-permute-done.8.near), channel_id=1, source_target_pairs={{0,96},{1,25},{8,104},{9,1},{16,112},{17,9},{24,120},{25,17},{32,0... | collective-permute-start | bytes 3145736 | tf_op jit(solution)/shard_map/ppermute | solution.py:372
  73.5 0.0 collective-permute-start.11
  73.5 6.1 %shard_map.58.held = f32[1024,8,128]{2,1,0:T(8,128)S(1)} custom-call(bf16[2,1024,1024]{2,1,0:T(8,128)(2,1)S(1)} %get-tuple-element.24.f_ref, f32[256,1024]{1,0:T(8,128)S(1)} %collective-permute-done.8.near, f32[256,1024]{1,0:T(8,128)S(1)} %collective-permute-done.9.far, f32[1024,16,128]{2,1,0:T(8,128)} %bitcast.13), custom_call_target="tpu_custom_call" | custom-call | flops 2000000000 | bytes 1048576 | tf_op jit(solution)/shard_map/pallas_call | solution.py:52
  79.6 1.5 %collective-permute-done.12.near = f32[256,1024]{1,0:T(8,128)S(1)} collective-permute-done((f32[256,1024]{1,0:T(8,128)S(1)}, f32[256,1024]{1,0:T(8,128)S(1)}, u32[]{:S(2)}, u32[]{:S(2)}) %collective-permute-start.12) | collective-permute-done | bytes 1048608 | tf_op jit(solution)/shard_map/ppermute | solution.py:369
  81.1 0.4 collective-permute-done.13.far
  81.5 5.4 %shard_map.59.rest_0_ = f32[1024,16,128]{2,1,0:T(8,128)} custom-call(bf16[2,1024,1024]{2,1,0:T(8,128)(2,1)S(1)} %get-tuple-element.24.f_ref, f32[256,1024]{1,0:T(8,128)S(1)} %collective-permute-done.12.near, f32[256,1024]{1,0:T(8,128)S(1)} %collective-permute-done.13.far, f32[1024,8,128]{2,1,0:T(8,128)S(1)} %shard_map.58.held), custom_call_target="tpu_custom_call" | custom-call | flops 2000000000 | bytes 1048576 | tf_op jit(solution)/shard_map/pallas_call | solution.py:52
  86.9 5.5 %collective-permute-done.10.near = f32[256,1024]{1,0:T(8,128)S(1)} collective-permute-done((f32[256,1024]{1,0:T(8,128)S(1)}, f32[256,1024]{1,0:T(8,128)S(1)}, u32[]{:S(2)}, u32[]{:S(2)}) %collective-permute-start.10) | collective-permute-done | bytes 1048608 | tf_op jit(solution)/shard_map/ppermute | solution.py:372
  92.3 0.4 collective-permute-done.11.far
  92.7 5.4 %shard_map.60 = f32[1024,16,128]{2,1,0:T(8,128)} custom-call(bf16[2,1024,1024]{2,1,0:T(8,128)(2,1)S(1)} %get-tuple-element.24.f_ref, f32[256,1024]{1,0:T(8,128)S(1)} %collective-permute-done.10.near, f32[256,1024]{1,0:T(8,128)S(1)} %collective-permute-done.11.far, f32[1024,8,128]{2,1,0:T(8,128)S(1)} %shard_map.57.held, ...), custom_call_target="tpu_custom_call", output_to_operand_aliasing={{}: (4, {})} | custom-call | flops 2000000000 | bytes 1048576 | tf_op jit(solution)/shard_map/pallas_call | solution.py:52
  (2 shorter events, 0.1 us)
Async XLA Ops:
  0.6 34.9 %copy-start = (f32[1024,1024]{1,0:T(8,128)S(1)}, f32[1024,1024]{1,0:T(8,128)}, u32[]{:S(2)}) copy-start(f32[1024,1024]{1,0:T(8,128)} %rest_4_.1) | copy-start | bytes 12582916
  0.6 18.8 %collective-permute-start.1 = (f32[1024,128]{1,0:T(8,128)}, f32[1024,128]{1,0:T(8,128)S(1)}, u32[]{:S(2)}, u32[]{:S(2)}) collective-permute-start(f32[1024,128]{1,0:T(8,128)} %bitcast.7), channel_id=1, source_target_pairs={{0,2},{1,3},{8,10},{9,11},{16,18},{17,19},{24,26},{25,27},{32,34},... | collective-permute-start | bytes 1572872 | tf_op jit(solution)/shard_map/ppermute | solution.py:343
  1.1 18.3 %collective-permute-start = (f32[1024,128]{1,0:T(8,128)}, f32[1024,128]{1,0:T(8,128)S(1)}, u32[]{:S(2)}, u32[]{:S(2)}) collective-permute-start(f32[1024,128]{1,0:T(8,128)} %bitcast.8), channel_id=1, source_target_pairs={{0,6},{1,7},{8,14},{9,15},{16,22},{17,23},{24,30},{25,31},{32,38},... | collective-permute-start | bytes 1572872 | tf_op jit(solution)/shard_map/ppermute | solution.py:342
  2.7 1.1 %copy-start.1 = (f32[2,1,512,128]{3,2,1,0:T(8,128)S(1)}, f32[2,1,512,128]{3,2,1,0:T(8,128)}, u32[]{:S(2)}) copy-start(f32[2,1,512,128]{3,2,1,0:T(8,128)} %param.4) | copy-start | bytes 1572868
  19.5 17.5 %collective-permute-start.6 = (f32[1024,128]{1,0:T(8,128)S(1)}, f32[1024,128]{1,0:T(8,128)S(1)}, u32[]{:S(2)}, u32[]{:S(2)}) collective-permute-start(f32[1024,128]{1,0:T(8,128)S(1)} %shard_map.52), channel_id=1, source_target_pairs={{0,6},{1,3},{8,14},{9,11},{16,22},{17,19},{24,30},{25,27},{32,38},... | collective-permute-start | bytes 1572872 | tf_op jit(solution)/shard_map/ppermute | solution.py:348
  35.6 1.6 %copy-start.2 = (f32[2,1,512,128]{3,2,1,0:T(8,128)S(1)}, f32[2,1,512,128]{3,2,1,0:T(8,128)}, u32[]{:S(2)}) copy-start(f32[2,1,512,128]{3,2,1,0:T(8,128)} %param.4) | copy-start | bytes 1572868
  37.1 4.8 %collective-permute-start.7 = (f32[3072,128]{1,0:T(8,128)S(1)}, f32[3072,128]{1,0:T(8,128)S(1)}, u32[]{:S(2)}, u32[]{:S(2)}) collective-permute-start(f32[3072,128]{1,0:T(8,128)S(1)} %shard_map.53.rest_2_), channel_id=1, source_target_pairs={{0,1},{1,0},{8,9},{9,8},{16,17},{17,16},{24,25},{25,24},{32,33},{3... | collective-permute-start | bytes 4718600 | tf_op jit(solution)/shard_map/ppermute | solution.py:360
  37.2 4.6 %collective-permute-start.5 = (f32[1024,128]{1,0:T(8,128)S(1)}, f32[1024,128]{1,0:T(8,128)S(1)}, u32[]{:S(2)}, u32[]{:S(2)}) collective-permute-start(f32[1024,128]{1,0:T(8,128)S(1)} %bitcast.10), channel_id=1, source_target_pairs={{0,1},{1,0},{8,9},{9,8},{16,17},{17,16},{24,25},{25,24},{32,33},{3... | collective-permute-start | bytes 1572872 | tf_op jit(solution)/shard_map/ppermute | solution.py:341
  37.7 12.4 %collective-permute-start.4 = (f32[128,1024]{1,0:T(8,128)S(1)}, f32[128,1024]{1,0:T(8,128)S(1)}, u32[]{:S(2)}, u32[]{:S(2)}) collective-permute-start(f32[128,1024]{1,0:T(8,128)S(1)} %shard_map.51.refs_0_), channel_id=1, source_target_pairs={{0,16},{1,65},{8,24},{9,73},{16,0},{17,81},{24,8},{25,89},{32,48},... | collective-permute-start | bytes 1572872 | tf_op jit(solution)/shard_map/ppermute | solution.py:354
  38.6 15.4 %collective-permute-start.3 = (f32[128,1024]{1,0:T(8,128)S(1)}, f32[128,1024]{1,0:T(8,128)S(1)}, u32[]{:S(2)}, u32[]{:S(2)}) collective-permute-start(f32[128,1024]{1,0:T(8,128)S(1)} %shard_map.51.refs_0_), channel_id=1, source_target_pairs={{0,8},{1,33},{8,16},{9,41},{16,24},{17,49},{24,0},{25,57},{32,40},... | collective-permute-start | bytes 1572872 | tf_op jit(solution)/shard_map/ppermute | solution.py:353
  39.4 14.6 %collective-permute-start.2 = (f32[128,1024]{1,0:T(8,128)S(1)}, f32[128,1024]{1,0:T(8,128)S(1)}, u32[]{:S(2)}, u32[]{:S(2)}) collective-permute-start(f32[128,1024]{1,0:T(8,128)S(1)} %shard_map.51.refs_0_), channel_id=1, source_target_pairs={{0,24},{1,97},{8,0},{9,105},{16,8},{17,113},{24,16},{25,121},{32,5... | collective-permute-start | bytes 1572872 | tf_op jit(solution)/shard_map/ppermute | solution.py:352
  54.2 16.1 %collective-permute-start.9 = (f32[256,1024]{1,0:T(8,128)S(1)}, f32[256,1024]{1,0:T(8,128)S(1)}, u32[]{:S(2)}, u32[]{:S(2)}) collective-permute-start(f32[256,1024]{1,0:T(8,128)S(1)} %shard_map.56.far), channel_id=1, source_target_pairs={{0,32},{1,9},{8,40},{9,17},{16,48},{17,25},{24,56},{25,1},{32,64},... | collective-permute-start | bytes 3145736 | tf_op jit(solution)/shard_map/ppermute | solution.py:368
  54.9 15.4 %collective-permute-start.8 = (f32[256,1024]{1,0:T(8,128)S(1)}, f32[256,1024]{1,0:T(8,128)S(1)}, u32[]{:S(2)}, u32[]{:S(2)}) collective-permute-start(f32[256,1024]{1,0:T(8,128)S(1)} %shard_map.55.near), channel_id=1, source_target_pairs={{0,96},{1,25},{8,104},{9,1},{16,112},{17,9},{24,120},{25,17},{32,0... | collective-permute-start | bytes 3145736 | tf_op jit(solution)/shard_map/ppermute | solution.py:365
  57.5 23.6 %collective-permute-start.12 = (f32[256,1024]{1,0:T(8,128)S(1)}, f32[256,1024]{1,0:T(8,128)S(1)}, u32[]{:S(2)}, u32[]{:S(2)}) collective-permute-start(f32[256,1024]{1,0:T(8,128)S(1)} %shard_map.56.far), channel_id=1, source_target_pairs={{0,96},{1,25},{8,104},{9,1},{16,112},{17,9},{24,120},{25,17},{32,0... | collective-permute-start | bytes 3145736 | tf_op jit(solution)/shard_map/ppermute | solution.py:369
  58.3 23.2 %collective-permute-start.13 = (f32[256,1024]{1,0:T(8,128)S(1)}, f32[256,1024]{1,0:T(8,128)S(1)}, u32[]{:S(2)}, u32[]{:S(2)}) collective-permute-start(f32[256,1024]{1,0:T(8,128)S(1)} %shard_map.55.near), channel_id=1, source_target_pairs={{0,32},{1,9},{8,40},{9,17},{16,48},{17,25},{24,56},{25,1},{32,64},... | collective-permute-start | bytes 3145736 | tf_op jit(solution)/shard_map/ppermute | solution.py:366
  70.3 22.1 %collective-permute-start.10 = (f32[256,1024]{1,0:T(8,128)S(1)}, f32[256,1024]{1,0:T(8,128)S(1)}, u32[]{:S(2)}, u32[]{:S(2)}) collective-permute-start(f32[256,1024]{1,0:T(8,128)S(1)} %collective-permute-done.8.near), channel_id=1, source_target_pairs={{0,96},{1,25},{8,104},{9,1},{16,112},{17,9},{24,120},{25,17},{32,0... | collective-permute-start | bytes 3145736 | tf_op jit(solution)/shard_map/ppermute | solution.py:372
  73.5 19.2 %collective-permute-start.11 = (f32[256,1024]{1,0:T(8,128)S(1)}, f32[256,1024]{1,0:T(8,128)S(1)}, u32[]{:S(2)}, u32[]{:S(2)}) collective-permute-start(f32[256,1024]{1,0:T(8,128)S(1)} %collective-permute-done.9.far), channel_id=1, source_target_pairs={{0,32},{1,9},{8,40},{9,17},{16,48},{17,25},{24,56},{25,1},{32,64},... | collective-permute-start | bytes 3145736 | tf_op jit(solution)/shard_map/ppermute | solution.py:373

commit v4 on v3

--- a/solution.py
+++ b/solution.py
@@ -189,26 +189,23 @@
     )
 
 
-NEAR, FAR = (0, 1), (3, 2)
-
-
 def sub_rows(sources):
     _, core, y, z = place()
     first, second = jnp.where(core == 0, z, y), jnp.where(core == 0, y, z)
     spot = []
-    for move, steps in sources:
-        p = (second + move) & 3
-        for step in steps:
-            q = (first + step) & 3
-            other = (q >> 1) * 4 + (p >> 1) * 2 + (q & 1)
-            spot.append(jnp.where(core == 0, (p >> 1) * 4 + q, other))
+    for move, step in sources:
+        p, q = (second + move) & 3, (first + step) & 3
+        other = (q >> 1) * 4 + (p >> 1) * 2 + (q & 1)
+        spot.append(jnp.where(core == 0, (p >> 1) * 4 + q, other))
     group = pl.multiple_of(((second + sources[0][0]) & 1) * 8, 8)
     return group, spot
 
 
 def split_pieces(pieces, chi, clo):
-    for at, ref in enumerate(pieces):
-        rows = slice(at * 256, (at + 1) * 256)
+    at = 0
+    for ref in pieces:
+        rows = slice(at, at + ref.shape[0])
+        at += ref.shape[0]
         high, low = split(ref[...])
         chi[rows, :] = high
         clo[rows, :] = low
@@ -218,7 +215,7 @@
     step = 256
     lines = pl.ds(m * step, step)
     flat = buf.reshape(buf.shape[0] * 8, 128)
-    for n in range(2):
+    for n in range(len(spot) // 2):
         cols = slice(n * 256, (n + 1) * 256)
         product = dot3((f_ref[0, lines, :], f_ref[1, lines, :]), (chi[cols, :], clo[cols, :]))
         for j in range(2):
@@ -226,24 +223,36 @@
             flat[spots, :] = flat[spots, :] - product[:, j * 128 : (j + 1) * 128]
 
 
-def open_kernel(sources, f_ref, near, far, a_ref, held, chi, clo, sems):
+def open_kernel(sources, f_ref, *rest):
+    *pieces, a_ref, buf, chi, clo, sems = rest
     group, spot = sub_rows(sources)
     copies = []
-    for m in range(held.shape[0] // 256):
+    for m in range(buf.shape[0] // 256):
         lines = pl.ds(m * 256, 256)
         here = a_ref.at[lines, pl.ds(group, 8), :]
-        copies.append(pltpu.make_async_copy(here, held.at[lines], sems.at[m]))
+        copies.append(pltpu.make_async_copy(here, buf.at[lines], sems.at[m]))
         copies[-1].start()
-    split_pieces((near, far), chi, clo)
+    split_pieces(pieces, chi, clo)
     for m, copy in enumerate(copies):
         copy.wait()
-        subtract(m, spot, f_ref, chi, clo, held)
-
-
-def close_kernel(sources, f_ref, near, far, held, *rest):
+        subtract(m, spot, f_ref, chi, clo, buf)
+
+
+def middle_kernel(sources, f_ref, *rest):
+    *pieces, held, buf, chi, clo, sems = rest
+    _, spot = sub_rows(sources)
+    split_pieces(pieces, chi, clo)
+    for m in range(buf.shape[0] // 256):
+        lines = pl.ds(m * 256, 256)
+        buf[lines] = held[lines]
+        subtract(m, spot, f_ref, chi, clo, buf)
+
+
+def close_kernel(sources, after, f_ref, *rest):
+    *pieces, held = rest[: -5 - after]
     out_ref, buf, chi, clo, sems = rest[-5:]
     group, spot = sub_rows(sources)
-    split_pieces((near, far), chi, clo)
+    split_pieces(pieces, chi, clo)
     copies = []
     for m in range(buf.shape[0] // 256):
         lines = pl.ds(m * 256, 256)
@@ -256,42 +265,58 @@
         copy.wait()
 
 
-def update_scratch(local, order):
+def update_scratch(sources, f):
+    _, local, order = f.shape
     return [
-        pltpu.VMEM((512, order), BF16),
-        pltpu.VMEM((512, order), BF16),
+        pltpu.VMEM((128 * len(sources), order), BF16),
+        pltpu.VMEM((128 * len(sources), order), BF16),
         pltpu.SemaphoreType.DMA((local // 256,)),
     ]
 
 
-def open_group(sources, f, pieces, trailing):
-    _, local, order = f.shape
+def open_group(sources, f, pieces, source):
+    local = f.shape[1]
+    fresh = source.shape[1] != 8
     return call(
-        functools.partial(open_kernel, sources),
+        functools.partial(open_kernel if fresh else middle_kernel, sources),
         jax.ShapeDtypeStruct((local, 8, 128), F32),
-        (f, *pieces, trailing),
-        [VMEM, VMEM, VMEM, ANY],
+        (f, *pieces, source),
+        [VMEM] * (1 + len(pieces)) + [ANY if fresh else VMEM],
         VMEM,
-        update_scratch(local, order),
+        update_scratch(sources, f),
         LIM,
-        GF_UPDATE,
+        GF_UPDATE * len(sources) / 4,
     )
 
 
 def close_group(sources, f, pieces, held, shape, so_far):
-    _, local, order = f.shape
     after = () if so_far is None else (so_far,)
     return call(
-        functools.partial(close_kernel, sources),
+        functools.partial(close_kernel, sources, len(after)),
         jax.ShapeDtypeStruct(shape, F32),
         (f, *pieces, held, *after),
-        [VMEM] * 4 + [ANY] * len(after),
+        [VMEM] * (2 + len(pieces)) + [ANY] * len(after),
         ANY,
-        [pltpu.VMEM((local, 8, 128), F32), *update_scratch(local, order)],
+        [pltpu.VMEM((f.shape[1], 8, 128), F32), *update_scratch(sources, f)],
         LIM,
-        GF_UPDATE,
-        {4: 0} if after else {},
-    )
+        GF_UPDATE * len(sources) / 4,
+        {2 + len(pieces): 0} if after else {},
+    )
+
+
+def halve_kernel(*refs):
+    half = len(refs) // 3
+    for at, ref in enumerate(refs[:half]):
+        rows = ref.shape[0] // 2
+        refs[half + 2 * at][...] = ref[:rows]
+        refs[half + 2 * at + 1][...] = ref[rows:]
+
+
+def halve(*blocks):
+    rows, cols = blocks[0].shape
+    count = 2 * len(blocks)
+    part = jax.ShapeDtypeStruct((rows // 2, cols), F32)
+    return call(halve_kernel, [part] * count, blocks, [VMEM] * len(blocks), [VMEM] * count, [], LIM, 0.1)
 
 
 def pick_kernel(even_ref, odd_ref, out_ref):
@@ -367,16 +392,21 @@
     far = join(behind, across)
     far_behind = lax.ppermute(far, BOTH, second_axis(1))
     far_ahead = lax.ppermute(far, BOTH, second_axis(-1))
-    held = open_group(((0, NEAR), (0, FAR)), f, (near, far), trailing)
+    held = open_group(((0, 0), (0, 1), (0, 3), (0, 2)), f, (near, far), trailing)
     near_ahead, far_behind, held = lax.optimization_barrier((near_ahead, far_behind, held))
-    near_across = lax.ppermute(near_ahead, BOTH, second_axis(-1))
-    far_across = lax.ppermute(far_behind, BOTH, second_axis(1))
-
-    beside = open_group(((1, NEAR), (3, FAR)), f, (near_ahead, far_behind), trailing)
-    pieces, shape = (far_ahead, near_behind), trailing.shape
-    updated = close_group(((1, FAR), (3, NEAR)), f, pieces, beside, shape, None)
-    pieces = (near_across, far_across)
-    updated = close_group(((2, NEAR), (2, FAR)), f, pieces, held, shape, updated)
+    relay = halve(near_ahead, far_behind)
+    own_across = lax.ppermute(relay[0], BOTH, second_axis(-1))
+    behind_across = lax.ppermute(relay[2], BOTH, second_axis(1))
+    spots = ((1, 0), (1, 1), (3, 3), (3, 2))
+    beside = open_group(spots, f, (near_ahead, far_behind), trailing)
+    ahead, across, beside = lax.optimization_barrier((relay[1], relay[3], beside))
+    ahead_across = lax.ppermute(ahead, BOTH, second_axis(-1))
+    across_across = lax.ppermute(across, BOTH, second_axis(1))
+    last = (own_across, behind_across, ahead_across, across_across)
+    spots, shape = ((1, 3), (1, 2), (3, 0), (3, 1)), trailing.shape
+    updated = close_group(spots, f, (far_ahead, near_behind), beside, shape, None)
+    held = open_group(((2, 0), (2, 3)), f, last[:2], held)
+    updated = close_group(((2, 1), (2, 2)), f, last[2:], held, shape, updated)
     return updated.reshape(trailing_block.shape), own_columns.reshape(panel_block.shape)
 
 

time: 98.7 us -> 97.4 us (0.987)
  waiting for transfers between devices: 16.2 us -> 11.1 us
  starting transfers between devices: 16.3 us -> 19.7 us
    ppermute x2 -> x4, starting transfers between devices: 3.24 us -> 6.63 us  [the longest x1 3.31 us: per_device(): ahead_across = lax.ppermute(ahead, BOTH, second_axis(-1))]
    ppermute x2 -> x4, waiting for transfers between devices: 5.85 us -> 2.54 us  [the longest x1 1.37 us: per_device(): ahead_across = lax.ppermute(ahead, BOTH, second_axis(-1))]
    ppermute x1, waiting for transfers between devices: 1.5 us -> 0.01 us  [per_device(): far_ahead = lax.ppermute(far, BOTH, second_axis(-1))]
    pallas_call x11 -> x13, Pallas kernels: 33 us -> 33.7 us  [call(): pl.pallas_call(kernel, out_shape=out_shape, in_specs=in_specs, out_specs=...]
  transfers between devices with their start and end apart: 14 -> 16, of which waited for: 6 -> 4; matrix products, arithmetic and copies ran while one was open for 0% -> 0% of each run, Pallas kernels for 28% -> 31%
where the time goes in v4:
time: 97.4 us; the launch traced here: 97.2 us
  Pallas kernels  33.7 us (35%)
  blocking collectives  30.8 us (32%)
  starting transfers between devices  19.7 us (20%)
  waiting for transfers between devices  11.1 us (11%)
  local copies, waits for them, and re-layouts  1.08 us (1%)
    pallas_call x13, Pallas kernels, call(): pl.pallas_call(kernel, out_shape=out_shape, in_specs=in_specs, out_specs=...  33.7 us
    all_to_all x1, blocking collectives, per_device(): lax.all_to_all(mine, 'row', 0, 0, axis_index_groups=halves, tiled=True)  15.6 us
    all_to_all x1, blocking collectives, per_device(): mine = lax.all_to_all(mine, 'col', 0, 0, tiled=True)  15.2 us
    ppermute x1, waiting for transfers between devices, per_device(): far_behind = lax.ppermute(far, BOTH, second_axis(1))  4.63 us
    ppermute x1, waiting for transfers between devices, per_device(): behind = lax.ppermute(own, BOTH, first_axis(1))  3.87 us
    ppermute x1, starting transfers between devices, per_device(): ahead_across = lax.ppermute(ahead, BOTH, second_axis(-1))  3.31 us
    ppermute x1, starting transfers between devices, per_device(): own_across = lax.ppermute(relay[0], BOTH, second_axis(-1))  3.3 us
    ppermute x1, starting transfers between devices, per_device(): near_ahead = lax.ppermute(near, BOTH, second_axis(-1))  2.62 us
  transfers between devices with their start and end apart: 16, of which 4 were waited for; matrix products, arithmetic and copies ran while one was open for 0% of the time, Pallas kernels for 31%

profile of v4, /device:TPU:6, one launch (start us, length us, event | category | flops | bytes accessed | tf_op | source)
XLA Modules:
  0.0 97.2 jit_solution(6517243250435843892)
XLA Ops:
  0.6 0.0 copy-start
  0.6 0.5 collective-permute-start.1
  1.1 1.6 %collective-permute-start = (f32[1024,128]{1,0:T(8,128)}, f32[1024,128]{1,0:T(8,128)S(1)}, u32[]{:S(2)}, u32[]{:S(2)}) collective-permute-start(f32[1024,128]{1,0:T(8,128)} %bitcast.8), channel_id=1, source_target_pairs={{0,6},{1,7},{8,14},{9,15},{16,22},{17,23},{24,30},{25,31},{32,38},... | collective-permute-start | bytes 1572872 | tf_op jit(solution)/shard_map/ppermute | solution.py:367
  2.7 1.1 %copy-done.1 = f32[2,1,512,128]{3,2,1,0:T(8,128)S(1)} copy-done((f32[2,1,512,128]{3,2,1,0:T(8,128)S(1)}, f32[2,1,512,128]{3,2,1,0:T(8,128)}, u32[]{:S(2)}) %copy-start.1) | copy-done | bytes 524312
  3.8 15.6 %all_to_all.10 = f32[8,128,128]{2,1,0:T(8,128)S(1)} all-to-all(f32[8,128,128]{2,1,0:T(8,128)S(1)} %shard_map.50), channel_id=1, replica_groups={{0,8,16,24,32,40,48,56},{64,72,80,88,96,104,112,120},{1,9,17,25,33,41,4..., dimensions={0} | all-to-all | bytes 1048576 | tf_op jit(solution)/shard_map/all_to_all | solution.py:371
  19.4 0.0 collective-permute-done.1.odd_ref.refs_1_
  19.4 0.0 collective-permute-done.even_ref.refs_0_
  19.5 0.9 collective-permute-start.6
  20.4 15.2 %all_to_all.11.rows_ref = f32[8,128,128]{2,1,0:T(8,128)S(1)} all-to-all(f32[8,128,128]{2,1,0:T(8,128)S(1)} %all_to_all.10), channel_id=1, replica_groups=mesh['row'=16,'col'=8] {'col'}, dimensions={0} | all-to-all | bytes 1048576 | tf_op jit(solution)/shard_map/all_to_all | solution.py:374
  35.6 0.0 copy-done
  35.6 1.4 %shard_map.51.refs_0_ = f32[128,1024]{1,0:T(8,128)S(1)} custom-call(f32[8,128,128]{2,1,0:T(8,128)S(1)} %all_to_all.11.rows_ref, f32[1024,1024]{1,0:T(8,128)S(1)} %copy-done), custom_call_target="tpu_custom_call" | custom-call | flops 500000000 | bytes 1048576 | tf_op jit(solution)/shard_map/pallas_call | solution.py:52
  37.0 0.0 collective-permute-done.6.refs_2_
  37.0 0.1 shard_map.53.rest_2_
  37.1 0.1 collective-permute-start.7
  37.2 0.5 collective-permute-start.5
  37.7 0.9 collective-permute-start.4
  38.6 0.8 collective-permute-start.3
  39.4 2.5 %collective-permute-start.2 = (f32[128,1024]{1,0:T(8,128)S(1)}, f32[128,1024]{1,0:T(8,128)S(1)}, u32[]{:S(2)}, u32[]{:S(2)}) collective-permute-start(f32[128,1024]{1,0:T(8,128)S(1)} %shard_map.51.refs_0_), channel_id=1, source_target_pairs={{0,24},{1,97},{8,0},{9,105},{16,8},{17,113},{24,16},{25,121},{32,5... | collective-permute-start | bytes 1572872 | tf_op jit(solution)/shard_map/ppermute | solution.py:377
  41.9 0.0 collective-permute-done.5.rest_1_
  41.9 0.0 collective-permute-done.7.rest_3_
  41.9 8.3 %shard_map.54 = (f32[1024,128]{1,0:T(8,128)}, bf16[2,1024,1024]{2,1,0:T(8,128)(2,1)S(1)}) custom-call(f32[1024,128]{1,0:T(8,128)S(1)} %bitcast.11, f32[1024,128]{1,0:T(8,128)S(1)} %collective-permute-done.5.rest_1_, f32[3072,128]{1,0:T(8,128)S(1)} %shard_map.53.rest_2_, f32[3072,128]{1,0:T(8,128)S(1)} %collective-permute-done.7.rest_3_, f32[1024,1024]{1,0:T(8,128)S(1)} %copy-done), custom_call_target="tpu_custom_call" | custom-call | flops 4000000000 | bytes 1048576 | tf_op jit(solution)/shard_map/pallas_call | solution.py:52
  50.1 0.0 collective-permute-done.4.refs_1_
  50.1 3.9 %collective-permute-done.3.refs_0_ = f32[128,1024]{1,0:T(8,128)S(1)} collective-permute-done((f32[128,1024]{1,0:T(8,128)S(1)}, f32[128,1024]{1,0:T(8,128)S(1)}, u32[]{:S(2)}, u32[]{:S(2)}) %collective-permute-start.3) | collective-permute-done | bytes 524320 | tf_op jit(solution)/shard_map/ppermute | solution.py:378
  54.0 0.0 collective-permute-done.2.refs_1_
  54.0 0.1 shard_map.55.rest_0_
  54.1 0.1 shard_map.56.rest_1_
  54.2 0.7 collective-permute-start.9
  54.9 2.6 %collective-permute-start.8 = (f32[256,1024]{1,0:T(8,128)S(1)}, f32[256,1024]{1,0:T(8,128)S(1)}, u32[]{:S(2)}, u32[]{:S(2)}) collective-permute-start(f32[256,1024]{1,0:T(8,128)S(1)} %shard_map.55.rest_0_), channel_id=1, source_target_pairs={{0,96},{1,25},{8,104},{9,1},{16,112},{17,9},{24,120},{25,17},{32,0... | collective-permute-start | bytes 3145736 | tf_op jit(solution)/shard_map/ppermute | solution.py:390
  57.5 0.8 collective-permute-start.14
  58.3 1.2 %collective-permute-start.15 = (f32[256,1024]{1,0:T(8,128)S(1)}, f32[256,1024]{1,0:T(8,128)S(1)}, u32[]{:S(2)}, u32[]{:S(2)}) collective-permute-start(f32[256,1024]{1,0:T(8,128)S(1)} %shard_map.55.rest_0_), channel_id=1, source_target_pairs={{0,32},{1,9},{8,40},{9,17},{16,48},{17,25},{24,56},{25,1},{32,64},... | collective-permute-start | bytes 3145736 | tf_op jit(solution)/shard_map/ppermute | solution.py:391
  59.5 6.1 %shard_map.57.rest_2_ = f32[1024,8,128]{2,1,0:T(8,128)S(1)} custom-call(bf16[2,1024,1024]{2,1,0:T(8,128)(2,1)S(1)} %get-tuple-element.31.f_ref, f32[256,1024]{1,0:T(8,128)S(1)} %shard_map.55.rest_0_, f32[256,1024]{1,0:T(8,128)S(1)} %shard_map.56.rest_1_, f32[1024,16,128]{2,1,0:T(8,128)} %bitcast.13), custom_call_target="tpu_custom_call" | custom-call | flops 2000000000 | bytes 1048576 | tf_op jit(solution)/shard_map/pallas_call | solution.py:52
  65.6 4.6 %collective-permute-done.9.refs_1_.rest_1_ = f32[256,1024]{1,0:T(8,128)S(1)} collective-permute-done((f32[256,1024]{1,0:T(8,128)S(1)}, f32[256,1024]{1,0:T(8,128)S(1)}, u32[]{:S(2)}, u32[]{:S(2)}) %collective-permute-start.9) | collective-permute-done | bytes 1048608 | tf_op jit(solution)/shard_map/ppermute | solution.py:393
  70.2 0.0 collective-permute-done.8.refs_0_.rest_0_
  70.3 0.1 shard_map.58
  70.4 3.3 %collective-permute-start.12 = (f32[128,1024]{1,0:T(8,128)S(1)}, f32[128,1024]{1,0:T(8,128)S(1)}, u32[]{:S(2)}, u32[]{:S(2)}) collective-permute-start(f32[128,1024]{1,0:T(8,128)S(1)} %get-tuple-element.41), channel_id=1, source_target_pairs={{0,96},{1,25},{8,104},{9,1},{16,112},{17,9},{24,120},{25,17},{32,0... | collective-permute-start | bytes 1572872 | tf_op jit(solution)/shard_map/ppermute | solution.py:398
  73.7 0.0 collective-permute-start.13
  73.7 6.1 %shard_map.59.rest_2_ = f32[1024,8,128]{2,1,0:T(8,128)S(1)} custom-call(bf16[2,1024,1024]{2,1,0:T(8,128)(2,1)S(1)} %get-tuple-element.31.f_ref, f32[256,1024]{1,0:T(8,128)S(1)} %collective-permute-done.8.refs_0_.rest_0_, f32[256,1024]{1,0:T(8,128)S(1)} %collective-permute-done.9.refs_1_.rest_1_, f32[1024,16,128]{2,1,0:T(8,128)} %bitcast.14), custom_call_target="tpu_custom_call" | custom-call | flops 2000000000 | bytes 1048576 | tf_op jit(solution)/shard_map/pallas_call | solution.py:52
  79.8 3.3 %collective-permute-start.10 = (f32[128,1024]{1,0:T(8,128)S(1)}, f32[128,1024]{1,0:T(8,128)S(1)}, u32[]{:S(2)}, u32[]{:S(2)}) collective-permute-start(f32[128,1024]{1,0:T(8,128)S(1)} %get-tuple-element.39), channel_id=1, source_target_pairs={{0,96},{1,25},{8,104},{9,1},{16,112},{17,9},{24,120},{25,17},{32,0... | collective-permute-start | bytes 1572872 | tf_op jit(solution)/shard_map/ppermute | solution.py:403
  83.1 0.0 collective-permute-done.14.rest_0_
  83.1 0.0 collective-permute-start.11
  83.1 0.0 collective-permute-done.15.rest_1_
  83.1 5.4 %shard_map.61.rest_3_ = f32[1024,16,128]{2,1,0:T(8,128)} custom-call(bf16[2,1024,1024]{2,1,0:T(8,128)(2,1)S(1)} %get-tuple-element.31.f_ref, f32[256,1024]{1,0:T(8,128)S(1)} %collective-permute-done.14.rest_0_, f32[256,1024]{1,0:T(8,128)S(1)} %collective-permute-done.15.rest_1_, f32[1024,8,128]{2,1,0:T(8,128)S(1)} %shard_map.59.rest_2_), custom_call_target="tpu_custom_call" | custom-call | flops 2000000000 | bytes 1048576 | tf_op jit(solution)/shard_map/pallas_call | solution.py:52
  88.5 0.0 collective-permute-done.12.rest_0_
  88.5 0.0 collective-permute-done.13.rest_1_
  88.5 2.4 %shard_map.60.rest_2_ = f32[1024,8,128]{2,1,0:T(8,128)S(1)} custom-call(bf16[2,1024,1024]{2,1,0:T(8,128)(2,1)S(1)} %get-tuple-element.31.f_ref, f32[128,1024]{1,0:T(8,128)S(1)} %collective-permute-done.12.rest_0_, f32[128,1024]{1,0:T(8,128)S(1)} %collective-permute-done.13.rest_1_, f32[1024,8,128]{2,1,0:T(8,128)S(1)} %shard_map.57.rest_2_), custom_call_target="tpu_custom_call" | custom-call | flops 1000000000 | bytes 1048576 | tf_op jit(solution)/shard_map/pallas_call | solution.py:52
  91.0 1.4 %collective-permute-done.10.rest_0_ = f32[128,1024]{1,0:T(8,128)S(1)} collective-permute-done((f32[128,1024]{1,0:T(8,128)S(1)}, f32[128,1024]{1,0:T(8,128)S(1)}, u32[]{:S(2)}, u32[]{:S(2)}) %collective-permute-start.10) | collective-permute-done | bytes 524320 | tf_op jit(solution)/shard_map/ppermute | solution.py:403
  92.3 1.2 %collective-permute-done.11.rest_1_ = f32[128,1024]{1,0:T(8,128)S(1)} collective-permute-done((f32[128,1024]{1,0:T(8,128)S(1)}, f32[128,1024]{1,0:T(8,128)S(1)}, u32[]{:S(2)}, u32[]{:S(2)}) %collective-permute-start.11) | collective-permute-done | bytes 524320 | tf_op jit(solution)/shard_map/ppermute | solution.py:404
  93.5 3.5 %shard_map.62 = f32[1024,16,128]{2,1,0:T(8,128)} custom-call(bf16[2,1024,1024]{2,1,0:T(8,128)(2,1)S(1)} %get-tuple-element.31.f_ref, f32[128,1024]{1,0:T(8,128)S(1)} %collective-permute-done.10.rest_0_, f32[128,1024]{1,0:T(8,128)S(1)} %collective-permute-done.11.rest_1_, f32[1024,8,128]{2,1,0:T(8,128)S(1)} %shard_map.60.rest_2_, ...), custom_call_target="tpu_custom_call", output_to_operand_aliasing={{}: (4, {})} | custom-call | flops 1000000000 | bytes 1048576 | tf_op jit(solution)/shard_map/pallas_call | solution.py:52
  (5 shorter events, 0.1 us)
Async XLA Ops:
  0.6 34.9 %copy-start = (f32[1024,1024]{1,0:T(8,128)S(1)}, f32[1024,1024]{1,0:T(8,128)}, u32[]{:S(2)}) copy-start(f32[1024,1024]{1,0:T(8,128)} %rest_4_.1) | copy-start | bytes 12582916
  0.6 18.8 %collective-permute-start.1 = (f32[1024,128]{1,0:T(8,128)}, f32[1024,128]{1,0:T(8,128)S(1)}, u32[]{:S(2)}, u32[]{:S(2)}) collective-permute-start(f32[1024,128]{1,0:T(8,128)} %bitcast.7), channel_id=1, source_target_pairs={{0,2},{1,3},{8,10},{9,11},{16,18},{17,19},{24,26},{25,27},{32,34},... | collective-permute-start | bytes 1572872 | tf_op jit(solution)/shard_map/ppermute | solution.py:368
  1.1 18.3 %collective-permute-start = (f32[1024,128]{1,0:T(8,128)}, f32[1024,128]{1,0:T(8,128)S(1)}, u32[]{:S(2)}, u32[]{:S(2)}) collective-permute-start(f32[1024,128]{1,0:T(8,128)} %bitcast.8), channel_id=1, source_target_pairs={{0,6},{1,7},{8,14},{9,15},{16,22},{17,23},{24,30},{25,31},{32,38},... | collective-permute-start | bytes 1572872 | tf_op jit(solution)/shard_map/ppermute | solution.py:367
  2.7 1.1 %copy-start.1 = (f32[2,1,512,128]{3,2,1,0:T(8,128)S(1)}, f32[2,1,512,128]{3,2,1,0:T(8,128)}, u32[]{:S(2)}) copy-start(f32[2,1,512,128]{3,2,1,0:T(8,128)} %param.4) | copy-start | bytes 1572868
  19.5 17.5 %collective-permute-start.6 = (f32[1024,128]{1,0:T(8,128)S(1)}, f32[1024,128]{1,0:T(8,128)S(1)}, u32[]{:S(2)}, u32[]{:S(2)}) collective-permute-start(f32[1024,128]{1,0:T(8,128)S(1)} %shard_map.52), channel_id=1, source_target_pairs={{0,6},{1,3},{8,14},{9,11},{16,22},{17,19},{24,30},{25,27},{32,38},... | collective-permute-start | bytes 1572872 | tf_op jit(solution)/shard_map/ppermute | solution.py:373
  35.6 1.6 %copy-start.2 = (f32[2,1,512,128]{3,2,1,0:T(8,128)S(1)}, f32[2,1,512,128]{3,2,1,0:T(8,128)}, u32[]{:S(2)}) copy-start(f32[2,1,512,128]{3,2,1,0:T(8,128)} %param.4) | copy-start | bytes 1572868
  37.1 4.8 %collective-permute-start.7 = (f32[3072,128]{1,0:T(8,128)S(1)}, f32[3072,128]{1,0:T(8,128)S(1)}, u32[]{:S(2)}, u32[]{:S(2)}) collective-permute-start(f32[3072,128]{1,0:T(8,128)S(1)} %shard_map.53.rest_2_), channel_id=1, source_target_pairs={{0,1},{1,0},{8,9},{9,8},{16,17},{17,16},{24,25},{25,24},{32,33},{3... | collective-permute-start | bytes 4718600 | tf_op jit(solution)/shard_map/ppermute | solution.py:385
  37.2 4.6 %collective-permute-start.5 = (f32[1024,128]{1,0:T(8,128)S(1)}, f32[1024,128]{1,0:T(8,128)S(1)}, u32[]{:S(2)}, u32[]{:S(2)}) collective-permute-start(f32[1024,128]{1,0:T(8,128)S(1)} %bitcast.10), channel_id=1, source_target_pairs={{0,1},{1,0},{8,9},{9,8},{16,17},{17,16},{24,25},{25,24},{32,33},{3... | collective-permute-start | bytes 1572872 | tf_op jit(solution)/shard_map/ppermute | solution.py:366
  37.7 12.4 %collective-permute-start.4 = (f32[128,1024]{1,0:T(8,128)S(1)}, f32[128,1024]{1,0:T(8,128)S(1)}, u32[]{:S(2)}, u32[]{:S(2)}) collective-permute-start(f32[128,1024]{1,0:T(8,128)S(1)} %shard_map.51.refs_0_), channel_id=1, source_target_pairs={{0,16},{1,65},{8,24},{9,73},{16,0},{17,81},{24,8},{25,89},{32,48},... | collective-permute-start | bytes 1572872 | tf_op jit(solution)/shard_map/ppermute | solution.py:379
  38.6 15.4 %collective-permute-start.3 = (f32[128,1024]{1,0:T(8,128)S(1)}, f32[128,1024]{1,0:T(8,128)S(1)}, u32[]{:S(2)}, u32[]{:S(2)}) collective-permute-start(f32[128,1024]{1,0:T(8,128)S(1)} %shard_map.51.refs_0_), channel_id=1, source_target_pairs={{0,8},{1,33},{8,16},{9,41},{16,24},{17,49},{24,0},{25,57},{32,40},... | collective-permute-start | bytes 1572872 | tf_op jit(solution)/shard_map/ppermute | solution.py:378
  39.4 14.6 %collective-permute-start.2 = (f32[128,1024]{1,0:T(8,128)S(1)}, f32[128,1024]{1,0:T(8,128)S(1)}, u32[]{:S(2)}, u32[]{:S(2)}) collective-permute-start(f32[128,1024]{1,0:T(8,128)S(1)} %shard_map.51.refs_0_), channel_id=1, source_target_pairs={{0,24},{1,97},{8,0},{9,105},{16,8},{17,113},{24,16},{25,121},{32,5... | collective-permute-start | bytes 1572872 | tf_op jit(solution)/shard_map/ppermute | solution.py:377
  54.2 16.1 %collective-permute-start.9 = (f32[256,1024]{1,0:T(8,128)S(1)}, f32[256,1024]{1,0:T(8,128)S(1)}, u32[]{:S(2)}, u32[]{:S(2)}) collective-permute-start(f32[256,1024]{1,0:T(8,128)S(1)} %shard_map.56.rest_1_), channel_id=1, source_target_pairs={{0,32},{1,9},{8,40},{9,17},{16,48},{17,25},{24,56},{25,1},{32,64},... | collective-permute-start | bytes 3145736 | tf_op jit(solution)/shard_map/ppermute | solution.py:393
  54.9 15.4 %collective-permute-start.8 = (f32[256,1024]{1,0:T(8,128)S(1)}, f32[256,1024]{1,0:T(8,128)S(1)}, u32[]{:S(2)}, u32[]{:S(2)}) collective-permute-start(f32[256,1024]{1,0:T(8,128)S(1)} %shard_map.55.rest_0_), channel_id=1, source_target_pairs={{0,96},{1,25},{8,104},{9,1},{16,112},{17,9},{24,120},{25,17},{32,0... | collective-permute-start | bytes 3145736 | tf_op jit(solution)/shard_map/ppermute | solution.py:390
  57.5 25.6 %collective-permute-start.14 = (f32[256,1024]{1,0:T(8,128)S(1)}, f32[256,1024]{1,0:T(8,128)S(1)}, u32[]{:S(2)}, u32[]{:S(2)}) collective-permute-start(f32[256,1024]{1,0:T(8,128)S(1)} %shard_map.56.rest_1_), channel_id=1, source_target_pairs={{0,96},{1,25},{8,104},{9,1},{16,112},{17,9},{24,120},{25,17},{32,0... | collective-permute-start | bytes 3145736 | tf_op jit(solution)/shard_map/ppermute | solution.py:394
  58.3 24.8 %collective-permute-start.15 = (f32[256,1024]{1,0:T(8,128)S(1)}, f32[256,1024]{1,0:T(8,128)S(1)}, u32[]{:S(2)}, u32[]{:S(2)}) collective-permute-start(f32[256,1024]{1,0:T(8,128)S(1)} %shard_map.55.rest_0_), channel_id=1, source_target_pairs={{0,32},{1,9},{8,40},{9,17},{16,48},{17,25},{24,56},{25,1},{32,64},... | collective-permute-start | bytes 3145736 | tf_op jit(solution)/shard_map/ppermute | solution.py:391
  70.4 18.1 %collective-permute-start.12 = (f32[128,1024]{1,0:T(8,128)S(1)}, f32[128,1024]{1,0:T(8,128)S(1)}, u32[]{:S(2)}, u32[]{:S(2)}) collective-permute-start(f32[128,1024]{1,0:T(8,128)S(1)} %get-tuple-element.41), channel_id=1, source_target_pairs={{0,96},{1,25},{8,104},{9,1},{16,112},{17,9},{24,120},{25,17},{32,0... | collective-permute-start | bytes 1572872 | tf_op jit(solution)/shard_map/ppermute | solution.py:398
  73.7 14.8 %collective-permute-start.13 = (f32[128,1024]{1,0:T(8,128)S(1)}, f32[128,1024]{1,0:T(8,128)S(1)}, u32[]{:S(2)}, u32[]{:S(2)}) collective-permute-start(f32[128,1024]{1,0:T(8,128)S(1)} %get-tuple-element.42), channel_id=1, source_target_pairs={{0,32},{1,9},{8,40},{9,17},{16,48},{17,25},{24,56},{25,1},{32,64},... | collective-permute-start | bytes 1572872 | tf_op jit(solution)/shard_map/ppermute | solution.py:399
  79.8 12.5 %collective-permute-start.10 = (f32[128,1024]{1,0:T(8,128)S(1)}, f32[128,1024]{1,0:T(8,128)S(1)}, u32[]{:S(2)}, u32[]{:S(2)}) collective-permute-start(f32[128,1024]{1,0:T(8,128)S(1)} %get-tuple-element.39), channel_id=1, source_target_pairs={{0,96},{1,25},{8,104},{9,1},{16,112},{17,9},{24,120},{25,17},{32,0... | collective-permute-start | bytes 1572872 | tf_op jit(solution)/shard_map/ppermute | solution.py:403
  83.1 10.4 %collective-permute-start.11 = (f32[128,1024]{1,0:T(8,128)S(1)}, f32[128,1024]{1,0:T(8,128)S(1)}, u32[]{:S(2)}, u32[]{:S(2)}) collective-permute-start(f32[128,1024]{1,0:T(8,128)S(1)} %get-tuple-element.40), channel_id=1, source_target_pairs={{0,32},{1,9},{8,40},{9,17},{16,48},{17,25},{24,56},{25,1},{32,64},... | collective-permute-start | bytes 1572872 | tf_op jit(solution)/shard_map/ppermute | solution.py:404

commit v5 on v4

--- a/solution.py
+++ b/solution.py
@@ -11,7 +11,7 @@
 F32, BF16 = jnp.float32, jnp.bfloat16
 LAST = (((1,), (1,)), ((), ()))
 GF_FACTOR, GF_UPDATE = 4.0, 2.0
-LIM = 40
+LIM = 38
 
 
 def permutation(move):

time: 97.4 us -> 97.4 us (level)
  no operation moved by 1% of the time
where the time goes in v5:
time: 97.4 us; the launch traced here: 97.2 us
  Pallas kernels  33.7 us (35%)
  blocking collectives  30.8 us (32%)
  starting transfers between devices  19.7 us (20%)
  waiting for transfers between devices  11.1 us (11%)
  local copies, waits for them, and re-layouts  1.08 us (1%)
    pallas_call x13, Pallas kernels, call(): pl.pallas_call(kernel, out_shape=out_shape, in_specs=in_specs, out_specs=...  33.7 us
    all_to_all x1, blocking collectives, per_device(): lax.all_to_all(mine, 'row', 0, 0, axis_index_groups=halves, tiled=True)  15.6 us
    all_to_all x1, blocking collectives, per_device(): mine = lax.all_to_all(mine, 'col', 0, 0, tiled=True)  15.2 us
    ppermute x1, waiting for transfers between devices, per_device(): far_behind = lax.ppermute(far, BOTH, second_axis(1))  4.63 us
    ppermute x1, waiting for transfers between devices, per_device(): behind = lax.ppermute(own, BOTH, first_axis(1))  3.87 us
    ppermute x1, starting transfers between devices, per_device(): ahead_across = lax.ppermute(ahead, BOTH, second_axis(-1))  3.31 us
    ppermute x1, starting transfers between devices, per_device(): own_across = lax.ppermute(relay[0], BOTH, second_axis(-1))  3.3 us
    ppermute x1, starting transfers between devices, per_device(): near_ahead = lax.ppermute(near, BOTH, second_axis(-1))  2.62 us
  transfers between devices with their start and end apart: 16, of which 4 were waited for; matrix products, arithmetic and copies ran while one was open for 0% of the time, Pallas kernels for 31%

profile of v5, /device:TPU:6, one launch (start us, length us, event | category | flops | bytes accessed | tf_op | source)
XLA Modules:
  0.0 97.2 jit_solution(13087505179571118436)
XLA Ops:
  0.6 0.0 copy-start
  0.6 0.5 collective-permute-start.1
  1.1 1.6 %collective-permute-start = (f32[1024,128]{1,0:T(8,128)}, f32[1024,128]{1,0:T(8,128)S(1)}, u32[]{:S(2)}, u32[]{:S(2)}) collective-permute-start(f32[1024,128]{1,0:T(8,128)} %bitcast.8), channel_id=1, source_target_pairs={{0,6},{1,7},{8,14},{9,15},{16,22},{17,23},{24,30},{25,31},{32,38},... | collective-permute-start | bytes 1572872 | tf_op jit(solution)/shard_map/ppermute | solution.py:367
  2.7 1.1 %copy-done.1 = f32[2,1,512,128]{3,2,1,0:T(8,128)S(1)} copy-done((f32[2,1,512,128]{3,2,1,0:T(8,128)S(1)}, f32[2,1,512,128]{3,2,1,0:T(8,128)}, u32[]{:S(2)}) %copy-start.1) | copy-done | bytes 524312
  3.8 15.6 %all_to_all.10 = f32[8,128,128]{2,1,0:T(8,128)S(1)} all-to-all(f32[8,128,128]{2,1,0:T(8,128)S(1)} %shard_map.50), channel_id=1, replica_groups={{0,8,16,24,32,40,48,56},{64,72,80,88,96,104,112,120},{1,9,17,25,33,41,4..., dimensions={0} | all-to-all | bytes 1048576 | tf_op jit(solution)/shard_map/all_to_all | solution.py:371
  19.4 0.0 collective-permute-done.1.odd_ref.refs_1_
  19.4 0.0 collective-permute-done.even_ref.refs_0_
  19.5 0.9 collective-permute-start.6
  20.4 15.2 %all_to_all.11.rows_ref = f32[8,128,128]{2,1,0:T(8,128)S(1)} all-to-all(f32[8,128,128]{2,1,0:T(8,128)S(1)} %all_to_all.10), channel_id=1, replica_groups=mesh['row'=16,'col'=8] {'col'}, dimensions={0} | all-to-all | bytes 1048576 | tf_op jit(solution)/shard_map/all_to_all | solution.py:374
  35.6 0.0 copy-done
  35.6 1.4 %shard_map.51.refs_0_ = f32[128,1024]{1,0:T(8,128)S(1)} custom-call(f32[8,128,128]{2,1,0:T(8,128)S(1)} %all_to_all.11.rows_ref, f32[1024,1024]{1,0:T(8,128)S(1)} %copy-done), custom_call_target="tpu_custom_call" | custom-call | flops 500000000 | bytes 1048576 | tf_op jit(solution)/shard_map/pallas_call | solution.py:52
  37.0 0.0 collective-permute-done.6.refs_2_
  37.0 0.1 shard_map.53.rest_2_
  37.1 0.1 collective-permute-start.7
  37.2 0.5 collective-permute-start.5
  37.7 0.9 collective-permute-start.4
  38.6 0.8 collective-permute-start.3
  39.4 2.5 %collective-permute-start.2 = (f32[128,1024]{1,0:T(8,128)S(1)}, f32[128,1024]{1,0:T(8,128)S(1)}, u32[]{:S(2)}, u32[]{:S(2)}) collective-permute-start(f32[128,1024]{1,0:T(8,128)S(1)} %shard_map.51.refs_0_), channel_id=1, source_target_pairs={{0,24},{1,97},{8,0},{9,105},{16,8},{17,113},{24,16},{25,121},{32,5... | collective-permute-start | bytes 1572872 | tf_op jit(solution)/shard_map/ppermute | solution.py:377
  41.9 0.0 collective-permute-done.5.rest_1_
  41.9 0.0 collective-permute-done.7.rest_3_
  41.9 8.3 %shard_map.54 = (f32[1024,128]{1,0:T(8,128)}, bf16[2,1024,1024]{2,1,0:T(8,128)(2,1)S(1)}) custom-call(f32[1024,128]{1,0:T(8,128)S(1)} %bitcast.11, f32[1024,128]{1,0:T(8,128)S(1)} %collective-permute-done.5.rest_1_, f32[3072,128]{1,0:T(8,128)S(1)} %shard_map.53.rest_2_, f32[3072,128]{1,0:T(8,128)S(1)} %collective-permute-done.7.rest_3_, f32[1024,1024]{1,0:T(8,128)S(1)} %copy-done), custom_call_target="tpu_custom_call" | custom-call | flops 4000000000 | bytes 1048576 | tf_op jit(solution)/shard_map/pallas_call | solution.py:52
  50.1 0.0 collective-permute-done.4.refs_1_
  50.1 3.9 %collective-permute-done.3.refs_0_ = f32[128,1024]{1,0:T(8,128)S(1)} collective-permute-done((f32[128,1024]{1,0:T(8,128)S(1)}, f32[128,1024]{1,0:T(8,128)S(1)}, u32[]{:S(2)}, u32[]{:S(2)}) %collective-permute-start.3) | collective-permute-done | bytes 524320 | tf_op jit(solution)/shard_map/ppermute | solution.py:378
  54.0 0.0 collective-permute-done.2.refs_1_
  54.0 0.1 shard_map.55.rest_0_
  54.1 0.1 shard_map.56.rest_1_
  54.2 0.7 collective-permute-start.9
  54.9 2.6 %collective-permute-start.8 = (f32[256,1024]{1,0:T(8,128)S(1)}, f32[256,1024]{1,0:T(8,128)S(1)}, u32[]{:S(2)}, u32[]{:S(2)}) collective-permute-start(f32[256,1024]{1,0:T(8,128)S(1)} %shard_map.55.rest_0_), channel_id=1, source_target_pairs={{0,96},{1,25},{8,104},{9,1},{16,112},{17,9},{24,120},{25,17},{32,0... | collective-permute-start | bytes 3145736 | tf_op jit(solution)/shard_map/ppermute | solution.py:390
  57.5 0.8 collective-permute-start.14
  58.3 1.2 %collective-permute-start.15 = (f32[256,1024]{1,0:T(8,128)S(1)}, f32[256,1024]{1,0:T(8,128)S(1)}, u32[]{:S(2)}, u32[]{:S(2)}) collective-permute-start(f32[256,1024]{1,0:T(8,128)S(1)} %shard_map.55.rest_0_), channel_id=1, source_target_pairs={{0,32},{1,9},{8,40},{9,17},{16,48},{17,25},{24,56},{25,1},{32,64},... | collective-permute-start | bytes 3145736 | tf_op jit(solution)/shard_map/ppermute | solution.py:391
  59.5 6.1 %shard_map.57.rest_2_ = f32[1024,8,128]{2,1,0:T(8,128)S(1)} custom-call(bf16[2,1024,1024]{2,1,0:T(8,128)(2,1)S(1)} %get-tuple-element.31.f_ref, f32[256,1024]{1,0:T(8,128)S(1)} %shard_map.55.rest_0_, f32[256,1024]{1,0:T(8,128)S(1)} %shard_map.56.rest_1_, f32[1024,16,128]{2,1,0:T(8,128)} %bitcast.13), custom_call_target="tpu_custom_call" | custom-call | flops 2000000000 | bytes 1048576 | tf_op jit(solution)/shard_map/pallas_call | solution.py:52
  65.6 4.6 %collective-permute-done.9.refs_1_.rest_1_ = f32[256,1024]{1,0:T(8,128)S(1)} collective-permute-done((f32[256,1024]{1,0:T(8,128)S(1)}, f32[256,1024]{1,0:T(8,128)S(1)}, u32[]{:S(2)}, u32[]{:S(2)}) %collective-permute-start.9) | collective-permute-done | bytes 1048608 | tf_op jit(solution)/shard_map/ppermute | solution.py:393
  70.2 0.0 collective-permute-done.8.refs_0_.rest_0_
  70.3 0.1 shard_map.58
  70.4 3.3 %collective-permute-start.12 = (f32[128,1024]{1,0:T(8,128)S(1)}, f32[128,1024]{1,0:T(8,128)S(1)}, u32[]{:S(2)}, u32[]{:S(2)}) collective-permute-start(f32[128,1024]{1,0:T(8,128)S(1)} %get-tuple-element.41), channel_id=1, source_target_pairs={{0,96},{1,25},{8,104},{9,1},{16,112},{17,9},{24,120},{25,17},{32,0... | collective-permute-start | bytes 1572872 | tf_op jit(solution)/shard_map/ppermute | solution.py:398
  73.7 0.0 collective-permute-start.13
  73.7 6.1 %shard_map.59.rest_2_ = f32[1024,8,128]{2,1,0:T(8,128)S(1)} custom-call(bf16[2,1024,1024]{2,1,0:T(8,128)(2,1)S(1)} %get-tuple-element.31.f_ref, f32[256,1024]{1,0:T(8,128)S(1)} %collective-permute-done.8.refs_0_.rest_0_, f32[256,1024]{1,0:T(8,128)S(1)} %collective-permute-done.9.refs_1_.rest_1_, f32[1024,16,128]{2,1,0:T(8,128)} %bitcast.14), custom_call_target="tpu_custom_call" | custom-call | flops 2000000000 | bytes 1048576 | tf_op jit(solution)/shard_map/pallas_call | solution.py:52
  79.8 3.3 %collective-permute-start.10 = (f32[128,1024]{1,0:T(8,128)S(1)}, f32[128,1024]{1,0:T(8,128)S(1)}, u32[]{:S(2)}, u32[]{:S(2)}) collective-permute-start(f32[128,1024]{1,0:T(8,128)S(1)} %get-tuple-element.39), channel_id=1, source_target_pairs={{0,96},{1,25},{8,104},{9,1},{16,112},{17,9},{24,120},{25,17},{32,0... | collective-permute-start | bytes 1572872 | tf_op jit(solution)/shard_map/ppermute | solution.py:403
  83.1 0.0 collective-permute-done.14.rest_0_
  83.1 0.0 collective-permute-start.11
  83.1 0.0 collective-permute-done.15.rest_1_
  83.1 5.4 %shard_map.61.rest_3_ = f32[1024,16,128]{2,1,0:T(8,128)} custom-call(bf16[2,1024,1024]{2,1,0:T(8,128)(2,1)S(1)} %get-tuple-element.31.f_ref, f32[256,1024]{1,0:T(8,128)S(1)} %collective-permute-done.14.rest_0_, f32[256,1024]{1,0:T(8,128)S(1)} %collective-permute-done.15.rest_1_, f32[1024,8,128]{2,1,0:T(8,128)S(1)} %shard_map.59.rest_2_), custom_call_target="tpu_custom_call" | custom-call | flops 2000000000 | bytes 1048576 | tf_op jit(solution)/shard_map/pallas_call | solution.py:52
  88.5 0.0 collective-permute-done.12.rest_0_
  88.5 0.0 collective-permute-done.13.rest_1_
  88.5 2.4 %shard_map.60.rest_2_ = f32[1024,8,128]{2,1,0:T(8,128)S(1)} custom-call(bf16[2,1024,1024]{2,1,0:T(8,128)(2,1)S(1)} %get-tuple-element.31.f_ref, f32[128,1024]{1,0:T(8,128)S(1)} %collective-permute-done.12.rest_0_, f32[128,1024]{1,0:T(8,128)S(1)} %collective-permute-done.13.rest_1_, f32[1024,8,128]{2,1,0:T(8,128)S(1)} %shard_map.57.rest_2_), custom_call_target="tpu_custom_call" | custom-call | flops 1000000000 | bytes 1048576 | tf_op jit(solution)/shard_map/pallas_call | solution.py:52
  91.0 1.4 %collective-permute-done.10.rest_0_ = f32[128,1024]{1,0:T(8,128)S(1)} collective-permute-done((f32[128,1024]{1,0:T(8,128)S(1)}, f32[128,1024]{1,0:T(8,128)S(1)}, u32[]{:S(2)}, u32[]{:S(2)}) %collective-permute-start.10) | collective-permute-done | bytes 524320 | tf_op jit(solution)/shard_map/ppermute | solution.py:403
  92.3 1.2 %collective-permute-done.11.rest_1_ = f32[128,1024]{1,0:T(8,128)S(1)} collective-permute-done((f32[128,1024]{1,0:T(8,128)S(1)}, f32[128,1024]{1,0:T(8,128)S(1)}, u32[]{:S(2)}, u32[]{:S(2)}) %collective-permute-start.11) | collective-permute-done | bytes 524320 | tf_op jit(solution)/shard_map/ppermute | solution.py:404
  93.5 3.5 %shard_map.62 = f32[1024,16,128]{2,1,0:T(8,128)} custom-call(bf16[2,1024,1024]{2,1,0:T(8,128)(2,1)S(1)} %get-tuple-element.31.f_ref, f32[128,1024]{1,0:T(8,128)S(1)} %collective-permute-done.10.rest_0_, f32[128,1024]{1,0:T(8,128)S(1)} %collective-permute-done.11.rest_1_, f32[1024,8,128]{2,1,0:T(8,128)S(1)} %shard_map.60.rest_2_, ...), custom_call_target="tpu_custom_call", output_to_operand_aliasing={{}: (4, {})} | custom-call | flops 1000000000 | bytes 1048576 | tf_op jit(solution)/shard_map/pallas_call | solution.py:52
  (5 shorter events, 0.1 us)
Async XLA Ops:
  0.6 34.9 %copy-start = (f32[1024,1024]{1,0:T(8,128)S(1)}, f32[1024,1024]{1,0:T(8,128)}, u32[]{:S(2)}) copy-start(f32[1024,1024]{1,0:T(8,128)} %rest_4_.1) | copy-start | bytes 12582916
  0.6 18.8 %collective-permute-start.1 = (f32[1024,128]{1,0:T(8,128)}, f32[1024,128]{1,0:T(8,128)S(1)}, u32[]{:S(2)}, u32[]{:S(2)}) collective-permute-start(f32[1024,128]{1,0:T(8,128)} %bitcast.7), channel_id=1, source_target_pairs={{0,2},{1,3},{8,10},{9,11},{16,18},{17,19},{24,26},{25,27},{32,34},... | collective-permute-start | bytes 1572872 | tf_op jit(solution)/shard_map/ppermute | solution.py:368
  1.1 18.3 %collective-permute-start = (f32[1024,128]{1,0:T(8,128)}, f32[1024,128]{1,0:T(8,128)S(1)}, u32[]{:S(2)}, u32[]{:S(2)}) collective-permute-start(f32[1024,128]{1,0:T(8,128)} %bitcast.8), channel_id=1, source_target_pairs={{0,6},{1,7},{8,14},{9,15},{16,22},{17,23},{24,30},{25,31},{32,38},... | collective-permute-start | bytes 1572872 | tf_op jit(solution)/shard_map/ppermute | solution.py:367
  2.7 1.1 %copy-start.1 = (f32[2,1,512,128]{3,2,1,0:T(8,128)S(1)}, f32[2,1,512,128]{3,2,1,0:T(8,128)}, u32[]{:S(2)}) copy-start(f32[2,1,512,128]{3,2,1,0:T(8,128)} %param.4) | copy-start | bytes 1572868
  19.5 17.5 %collective-permute-start.6 = (f32[1024,128]{1,0:T(8,128)S(1)}, f32[1024,128]{1,0:T(8,128)S(1)}, u32[]{:S(2)}, u32[]{:S(2)}) collective-permute-start(f32[1024,128]{1,0:T(8,128)S(1)} %shard_map.52), channel_id=1, source_target_pairs={{0,6},{1,3},{8,14},{9,11},{16,22},{17,19},{24,30},{25,27},{32,38},... | collective-permute-start | bytes 1572872 | tf_op jit(solution)/shard_map/ppermute | solution.py:373
  35.6 1.6 %copy-start.2 = (f32[2,1,512,128]{3,2,1,0:T(8,128)S(1)}, f32[2,1,512,128]{3,2,1,0:T(8,128)}, u32[]{:S(2)}) copy-start(f32[2,1,512,128]{3,2,1,0:T(8,128)} %param.4) | copy-start | bytes 1572868
  37.1 4.8 %collective-permute-start.7 = (f32[3072,128]{1,0:T(8,128)S(1)}, f32[3072,128]{1,0:T(8,128)S(1)}, u32[]{:S(2)}, u32[]{:S(2)}) collective-permute-start(f32[3072,128]{1,0:T(8,128)S(1)} %shard_map.53.rest_2_), channel_id=1, source_target_pairs={{0,1},{1,0},{8,9},{9,8},{16,17},{17,16},{24,25},{25,24},{32,33},{3... | collective-permute-start | bytes 4718600 | tf_op jit(solution)/shard_map/ppermute | solution.py:385
  37.2 4.6 %collective-permute-start.5 = (f32[1024,128]{1,0:T(8,128)S(1)}, f32[1024,128]{1,0:T(8,128)S(1)}, u32[]{:S(2)}, u32[]{:S(2)}) collective-permute-start(f32[1024,128]{1,0:T(8,128)S(1)} %bitcast.10), channel_id=1, source_target_pairs={{0,1},{1,0},{8,9},{9,8},{16,17},{17,16},{24,25},{25,24},{32,33},{3... | collective-permute-start | bytes 1572872 | tf_op jit(solution)/shard_map/ppermute | solution.py:366
  37.7 12.4 %collective-permute-start.4 = (f32[128,1024]{1,0:T(8,128)S(1)}, f32[128,1024]{1,0:T(8,128)S(1)}, u32[]{:S(2)}, u32[]{:S(2)}) collective-permute-start(f32[128,1024]{1,0:T(8,128)S(1)} %shard_map.51.refs_0_), channel_id=1, source_target_pairs={{0,16},{1,65},{8,24},{9,73},{16,0},{17,81},{24,8},{25,89},{32,48},... | collective-permute-start | bytes 1572872 | tf_op jit(solution)/shard_map/ppermute | solution.py:379
  38.6 15.4 %collective-permute-start.3 = (f32[128,1024]{1,0:T(8,128)S(1)}, f32[128,1024]{1,0:T(8,128)S(1)}, u32[]{:S(2)}, u32[]{:S(2)}) collective-permute-start(f32[128,1024]{1,0:T(8,128)S(1)} %shard_map.51.refs_0_), channel_id=1, source_target_pairs={{0,8},{1,33},{8,16},{9,41},{16,24},{17,49},{24,0},{25,57},{32,40},... | collective-permute-start | bytes 1572872 | tf_op jit(solution)/shard_map/ppermute | solution.py:378
  39.4 14.6 %collective-permute-start.2 = (f32[128,1024]{1,0:T(8,128)S(1)}, f32[128,1024]{1,0:T(8,128)S(1)}, u32[]{:S(2)}, u32[]{:S(2)}) collective-permute-start(f32[128,1024]{1,0:T(8,128)S(1)} %shard_map.51.refs_0_), channel_id=1, source_target_pairs={{0,24},{1,97},{8,0},{9,105},{16,8},{17,113},{24,16},{25,121},{32,5... | collective-permute-start | bytes 1572872 | tf_op jit(solution)/shard_map/ppermute | solution.py:377
  54.2 16.1 %collective-permute-start.9 = (f32[256,1024]{1,0:T(8,128)S(1)}, f32[256,1024]{1,0:T(8,128)S(1)}, u32[]{:S(2)}, u32[]{:S(2)}) collective-permute-start(f32[256,1024]{1,0:T(8,128)S(1)} %shard_map.56.rest_1_), channel_id=1, source_target_pairs={{0,32},{1,9},{8,40},{9,17},{16,48},{17,25},{24,56},{25,1},{32,64},... | collective-permute-start | bytes 3145736 | tf_op jit(solution)/shard_map/ppermute | solution.py:393
  54.9 15.4 %collective-permute-start.8 = (f32[256,1024]{1,0:T(8,128)S(1)}, f32[256,1024]{1,0:T(8,128)S(1)}, u32[]{:S(2)}, u32[]{:S(2)}) collective-permute-start(f32[256,1024]{1,0:T(8,128)S(1)} %shard_map.55.rest_0_), channel_id=1, source_target_pairs={{0,96},{1,25},{8,104},{9,1},{16,112},{17,9},{24,120},{25,17},{32,0... | collective-permute-start | bytes 3145736 | tf_op jit(solution)/shard_map/ppermute | solution.py:390
  57.5 25.6 %collective-permute-start.14 = (f32[256,1024]{1,0:T(8,128)S(1)}, f32[256,1024]{1,0:T(8,128)S(1)}, u32[]{:S(2)}, u32[]{:S(2)}) collective-permute-start(f32[256,1024]{1,0:T(8,128)S(1)} %shard_map.56.rest_1_), channel_id=1, source_target_pairs={{0,96},{1,25},{8,104},{9,1},{16,112},{17,9},{24,120},{25,17},{32,0... | collective-permute-start | bytes 3145736 | tf_op jit(solution)/shard_map/ppermute | solution.py:394
  58.3 24.8 %collective-permute-start.15 = (f32[256,1024]{1,0:T(8,128)S(1)}, f32[256,1024]{1,0:T(8,128)S(1)}, u32[]{:S(2)}, u32[]{:S(2)}) collective-permute-start(f32[256,1024]{1,0:T(8,128)S(1)} %shard_map.55.rest_0_), channel_id=1, source_target_pairs={{0,32},{1,9},{8,40},{9,17},{16,48},{17,25},{24,56},{25,1},{32,64},... | collective-permute-start | bytes 3145736 | tf_op jit(solution)/shard_map/ppermute | solution.py:391
  70.4 18.1 %collective-permute-start.12 = (f32[128,1024]{1,0:T(8,128)S(1)}, f32[128,1024]{1,0:T(8,128)S(1)}, u32[]{:S(2)}, u32[]{:S(2)}) collective-permute-start(f32[128,1024]{1,0:T(8,128)S(1)} %get-tuple-element.41), channel_id=1, source_target_pairs={{0,96},{1,25},{8,104},{9,1},{16,112},{17,9},{24,120},{25,17},{32,0... | collective-permute-start | bytes 1572872 | tf_op jit(solution)/shard_map/ppermute | solution.py:398
  73.7 14.8 %collective-permute-start.13 = (f32[128,1024]{1,0:T(8,128)S(1)}, f32[128,1024]{1,0:T(8,128)S(1)}, u32[]{:S(2)}, u32[]{:S(2)}) collective-permute-start(f32[128,1024]{1,0:T(8,128)S(1)} %get-tuple-element.42), channel_id=1, source_target_pairs={{0,32},{1,9},{8,40},{9,17},{16,48},{17,25},{24,56},{25,1},{32,64},... | collective-permute-start | bytes 1572872 | tf_op jit(solution)/shard_map/ppermute | solution.py:399
  79.8 12.5 %collective-permute-start.10 = (f32[128,1024]{1,0:T(8,128)S(1)}, f32[128,1024]{1,0:T(8,128)S(1)}, u32[]{:S(2)}, u32[]{:S(2)}) collective-permute-start(f32[128,1024]{1,0:T(8,128)S(1)} %get-tuple-element.39), channel_id=1, source_target_pairs={{0,96},{1,25},{8,104},{9,1},{16,112},{17,9},{24,120},{25,17},{32,0... | collective-permute-start | bytes 1572872 | tf_op jit(solution)/shard_map/ppermute | solution.py:403
  83.1 10.4 %collective-permute-start.11 = (f32[128,1024]{1,0:T(8,128)S(1)}, f32[128,1024]{1,0:T(8,128)S(1)}, u32[]{:S(2)}, u32[]{:S(2)}) collective-permute-start(f32[128,1024]{1,0:T(8,128)S(1)} %get-tuple-element.40), channel_id=1, source_target_pairs={{0,32},{1,9},{8,40},{9,17},{16,48},{17,25},{24,56},{25,1},{32,64},... | collective-permute-start | bytes 1572872 | tf_op jit(solution)/shard_map/ppermute | solution.py:404
